TPU v7x, 32 devices: a whole 2x2x4 slice. The times are simulated.
32 devices in a mesh: dp: 16 (over z, x, core), mp: 2 (over y).
Axes of the slice: x: 2, y: 2, z: 4, core: 2. Of those that a mesh axis runs over, the one named last changes fastest.
Arguments:
- tokens: bfloat16 [32768, 1024], P(('dp', 'mp')), may hold values from -6 to 6
- premix_gain: float32 [1024], replicated, may hold values from 0.5 to 1.5
- log_step: float32 [1024], P('mp'), may hold values from -6.9 to -2.3
- decay_rate: float32 [1024, 32], P('mp'), may hold values from 0.1 to 1
- frequency: float32 [1024, 32], P('mp'), may hold values from 0 to 100
- readout: float32 [2, 1024, 32], P(None, 'mp'), may hold values from -6 to 6
- skip_gain: float32 [1024], P('mp'), may hold values from -4 to 4
- prior_state: float32 [2, 32, 1024, 32], P(None, 'dp', 'mp'), may hold values from -1.2 to 1.2
- glu_weight: bfloat16 [1024, 2048], P('mp'), may hold values from -0.1875 to 0.1875
- preffn_gain: float32 [1024], replicated, may hold values from 0.5 to 1.5
- ffn_in: bfloat16 [1024, 4096], P(None, 'mp'), may hold values from -0.1875 to 0.1875
- ffn_out: bfloat16 [4096, 1024], P('mp'), may hold values from -0.1875 to 0.1875
- cotangent: bfloat16 [32768, 1024], P(('dp', 'mp')), may hold values from -6 to 6
Outputs:
- layer_out: bfloat16 [32768, 1024], P(('dp', 'mp'))
- tokens_grad: float32 [32768, 1024], P(('dp', 'mp'))
- premix_grad: float32 [1024], replicated
- logstep_grad: float32 [1024], P('mp')
- decay_grad: float32 [1024, 32], P('mp')
- frequency_grad: float32 [1024, 32], P('mp')
- readout_grad: float32 [2, 1024, 32], P(None, 'mp')
- skip_grad: float32 [1024], P('mp')
- state_grad: float32 [2, 32, 1024, 32], P(None, 'dp', 'mp')
- glu_grad: float32 [1024, 2048], P('mp')
- preffn_grad: float32 [1024], replicated
- ffnin_grad: float32 [1024, 4096], P(None, 'mp')
- ffnout_grad: float32 [4096, 1024], P('mp')
All inputs are finite; a program needn't handle non-finite values.
Results may differ from a plain program's by a relative error of at most 0.0085.
Values may be sent and summed in bfloat16 or wider, within the bound.
No kernel may reach another device: no remote copies, remote signals or barrier semaphores. Data moves between devices by JAX's collectives and lax.ppermute only.
A program may use at most 320 MiB of HBM per device.

v0:
```python
import math

import jax
import jax.numpy as jnp
from jax import lax
from jax.sharding import PartitionSpec as P

SEQ_LEN = 1024


MEDIUM = lax.Precision.HIGH
EPSILON = 1e-05


def layer_norm(values, gain):
    center = values - jnp.mean(values, axis=-1, keepdims=True)
    spread = jnp.mean(center * center, axis=-1, keepdims=True)
    return center * lax.rsqrt(spread + EPSILON) * gain


def gelu_exact(values):
    return jax.nn.gelu(values, approximate=False)


def fourier_tables(length):
    times = jnp.arange(length, dtype=jnp.int32)
    freqs = jnp.arange(2 * length, dtype=jnp.int32)
    phase = times[:, None] * freqs[None, :] % (2 * length)
    theta = phase.astype(jnp.float32) * (math.pi / length)
    return (jnp.cos(theta), jnp.sin(theta))


def mixer_local(
    mixin, log_step, decay_rate, frequency, readout, skip_gain, prior_state, cos_table, sin_table
):
    length = cos_table.shape[0]
    step = jnp.exp(log_step)[:, None]
    rate = decay_rate * step
    turn = frequency * step
    positions = jnp.arange(length, dtype=jnp.float32)
    magnitude = jnp.exp(-rate[:, :, None] * positions)
    angle = turn[:, :, None] * positions
    cos_pow = magnitude * jnp.cos(angle)
    sin_pow = magnitude * jnp.sin(angle)
    kernel = (
        2.0
        * step
        * (
            jnp.einsum("hm,hml->hl", readout[0], cos_pow, precision=MEDIUM)
            - jnp.einsum("hm,hml->hl", readout[1], sin_pow, precision=MEDIUM)
        )
    )
    decay = jnp.exp(-rate)
    zreal = decay * jnp.cos(turn)
    zimag = decay * jnp.sin(turn)
    sreal = readout[0] * prior_state[0] - readout[1] * prior_state[1]
    simag = readout[0] * prior_state[1] + readout[1] * prior_state[0]
    wreal = sreal * zreal - simag * zimag
    wimag = sreal * zimag + simag * zreal
    state_term = 2.0 * (
        jnp.einsum("shm,hml->slh", wreal, cos_pow, precision=MEDIUM)
        - jnp.einsum("shm,hml->slh", wimag, sin_pow, precision=MEDIUM)
    )
    in_real = jnp.einsum("slh,lf->shf", mixin, cos_table, precision=MEDIUM)
    in_imag = -jnp.einsum("slh,lf->shf", mixin, sin_table, precision=MEDIUM)
    ker_real = jnp.dot(kernel, cos_table, precision=MEDIUM)
    ker_imag = -jnp.dot(kernel, sin_table, precision=MEDIUM)
    out_real = in_real * ker_real - in_imag * ker_imag
    out_imag = in_real * ker_imag + in_imag * ker_real
    conv = (
        jnp.einsum("shf,lf->slh", out_real, cos_table, precision=MEDIUM)
        - jnp.einsum("shf,lf->slh", out_imag, sin_table, precision=MEDIUM)
    ) / (2.0 * length)
    return gelu_exact(conv + state_term + skip_gain * mixin)


def local(
    tokens,
    premix_gain,
    log_step,
    decay_rate,
    frequency,
    readout,
    skip_gain,
    prior_state,
    glu_weight,
    preffn_gain,
    ffn_in,
    ffn_out,
    cotangent,
):
    rows, width = tokens.shape
    channels = log_step.shape[0]
    group = rows * lax.axis_size("mp")
    segments = group // SEQ_LEN
    tok_float = tokens.astype(jnp.float32)
    normed, premix_pull = jax.vjp(layer_norm, tok_float, premix_gain)
    mixin = normed.astype(jnp.bfloat16)
    gathered = lax.all_gather(mixin, "mp", axis=0, tiled=True)
    own_mixin = lax.dynamic_slice_in_dim(gathered, lax.axis_index("mp") * channels, channels, 1)
    cos_table, sin_table = fourier_tables(SEQ_LEN)

    def mixer_piece(mix_rows, step_log, decays, freqs, coefs, skips, states):
        return mixer_local(
            mix_rows, step_log, decays, freqs, coefs, skips, states, cos_table, sin_table
        )

    mixed, mixer_pull = jax.vjp(
        mixer_piece,
        own_mixin.astype(jnp.float32).reshape(segments, SEQ_LEN, channels),
        log_step,
        decay_rate,
        frequency,
        readout,
        skip_gain,
        prior_state,
    )
    glu_in = mixed.reshape(group, channels).astype(jnp.bfloat16)
    pre_glu = lax.psum_scatter(
        jnp.dot(glu_in, glu_weight, preferred_element_type=jnp.float32),
        "mp",
        scatter_dimension=0,
        tiled=True,
    )
    value = pre_glu[:, :width]
    sigmoid_gate = jax.nn.sigmoid(pre_glu[:, width:])
    halfway = tok_float + value * sigmoid_gate
    ffn_normed, preffn_pull = jax.vjp(layer_norm, halfway, preffn_gain)
    ffn_input = lax.all_gather(ffn_normed.astype(jnp.bfloat16), "mp", axis=0, tiled=True)
    hidden = jnp.dot(ffn_input, ffn_in, preferred_element_type=jnp.float32)
    activated, gelu_pull = jax.vjp(gelu_exact, hidden)
    act_low = activated.astype(jnp.bfloat16)
    branch = lax.psum_scatter(
        jnp.dot(act_low, ffn_out, preferred_element_type=jnp.float32),
        "mp",
        scatter_dimension=0,
        tiled=True,
    )
    layer_out = (halfway + branch).astype(jnp.bfloat16)
    cot_rows = lax.all_gather(cotangent, "mp", axis=0, tiled=True)
    grad_ffn_out = jnp.einsum("lf,ld->fd", act_low, cot_rows, preferred_element_type=jnp.float32)
    grad_act = jnp.einsum("ld,fd->lf", cot_rows, ffn_out, preferred_element_type=jnp.float32)
    grad_hidden = gelu_pull(grad_act)[0].astype(jnp.bfloat16)
    grad_ffn_in = jnp.einsum(
        "ld,lf->df", ffn_input, grad_hidden, preferred_element_type=jnp.float32
    )
    grad_ffn_normed = lax.psum_scatter(
        jnp.einsum("lf,df->ld", grad_hidden, ffn_in, preferred_element_type=jnp.float32),
        "mp",
        scatter_dimension=0,
        tiled=True,
    )
    grad_half_norm, grad_preffn = preffn_pull(grad_ffn_normed)
    grad_halfway = cotangent.astype(jnp.float32) + grad_half_norm
    grad_value = grad_halfway * sigmoid_gate
    grad_gate = grad_halfway * value * sigmoid_gate * (1.0 - sigmoid_gate)
    grad_pre = jnp.concatenate([grad_value, grad_gate], axis=1).astype(jnp.bfloat16)
    grad_pre_rows = lax.all_gather(grad_pre, "mp", axis=0, tiled=True)
    grad_glu = jnp.einsum("lc,le->ce", glu_in, grad_pre_rows, preferred_element_type=jnp.float32)
    grad_glu_in = jnp.einsum(
        "le,ce->lc", grad_pre_rows, glu_weight, preferred_element_type=jnp.float32
    )
    mixer_grads = mixer_pull(grad_glu_in.reshape(segments, SEQ_LEN, channels))
    grad_mixin = mixer_grads[0].reshape(group, channels).astype(jnp.bfloat16)
    placed = jnp.zeros((group, width), jnp.float32)
    placed = lax.dynamic_update_slice_in_dim(
        placed, grad_mixin.astype(jnp.float32), lax.axis_index("mp") * channels, 1
    )
    grad_normed = lax.psum_scatter(
        placed.astype(jnp.bfloat16), "mp", scatter_dimension=0, tiled=True
    ).astype(jnp.float32)
    grad_tok_norm, grad_premix = premix_pull(grad_normed)
    tokens_grad = grad_halfway + grad_tok_norm
    grad_premix, grad_preffn = lax.psum((grad_premix, grad_preffn), ("dp", "mp"))
    grad_step, grad_decay, grad_freq, grad_readout, grad_skip, grad_state = mixer_grads[1:]
    (
        grad_glu,
        grad_ffn_in,
        grad_ffn_out,
        grad_step,
        grad_decay,
        grad_freq,
        grad_readout,
        grad_skip,
    ) = lax.psum(
        (
            grad_glu,
            grad_ffn_in,
            grad_ffn_out,
            grad_step,
            grad_decay,
            grad_freq,
            grad_readout,
            grad_skip,
        ),
        "dp",
    )
    return (
        layer_out,
        tokens_grad,
        grad_premix,
        grad_step,
        grad_decay,
        grad_freq,
        grad_readout,
        grad_skip,
        grad_state,
        grad_glu,
        grad_preffn,
        grad_ffn_in,
        grad_ffn_out,
    )


def solution(mesh):
    placed = (
        P(("dp", "mp"), None),
        P(),
        P("mp"),
        P("mp", None),
        P("mp", None),
        P(None, "mp", None),
        P("mp"),
        P(None, "dp", "mp", None),
        P("mp", None),
        P(),
        P(None, "mp"),
        P("mp", None),
        P(("dp", "mp"), None),
    )
    return jax.shard_map(
        local,
        mesh=mesh,
        in_specs=placed,
        out_specs=(
            P(("dp", "mp"), None),
            P(("dp", "mp"), None),
            P(),
            P("mp"),
            P("mp", None),
            P("mp", None),
            P(None, "mp", None),
            P("mp"),
            P(None, "dp", "mp", None),
            P("mp", None),
            P(),
            P(None, "mp"),
            P("mp", None),
        ),
        check_vma=False,
    )
```

profile of v0, /device:TPU:0, one launch (start us, length us, event | category | flops | bytes accessed | tf_op | source)
XLA Modules:
  0.0 4518.0 jit_solution(3416234856705500756)
XLA Ops:
  23.4 274.8 %fusion.8 = f32[512,1024,2]{1,2,0:T(2,128)} fusion(f32[512,32]{1,0:T(8,128)} %copy.96, f32[512,32]{1,0:T(8,128)} %copy.95, f32[2,512,32]{2,0,1:T(2,128)S(1)} %get-tuple-element.126, f32[2,512,32]{2,0,1:T(2,128)S(1)} %get-tuple-element.125, f32[512,32]{1,0:T(8,128)} %copy.103, f32[512,32]{1,0:T(8,128)} %copy.102), kind=kOutput, calls=%fused_computation.12 | convolution fusion | flops 251756544 | bytes 4718592 | tf_op jit(solution)/shard_map/jvp(shm,hml->slh)/dot_general | solution.py:62
  298.2 292.2 %fusion.16 = f32[512,1024,2]{1,2,0:T(2,128)} fusion(f32[512,32]{1,0:T(8,128)S(1)} %copy-done.51, f32[512,32]{1,0:T(8,128)S(1)} %copy-done.56, f32[2,512,32]{2,0,1:T(2,128)S(1)} %get-tuple-element.126, f32[2,512,32]{2,0,1:T(2,128)S(1)} %get-tuple-element.125, f32[512,32]{1,0:T(8,128)S(1)} %copy-done.39, f32[512,32]{1,0:T(8,128)S(1)} %copy-done.41), kind=kOutput, calls=%fused_computation.16 | convolution fusion | flops 251756544 | bytes 4718592 | tf_op jit(solution)/shard_map/jvp(shm,hml->slh)/dot_general | solution.py:61
  590.7 301.4 %fusion.10 = f32[512,1,1024]{2,1,0:T(1,128)} fusion(f32[512,32,1]{1,2,0:T(1,128)S(1)} %copy.127, f32[512,32]{1,0:T(8,128)} %copy.96, f32[512,32]{1,0:T(8,128)} %copy.95), kind=kOutput, calls=%fused_computation.13 | convolution fusion | flops 150994944 | bytes 2293760 | tf_op jit(solution)/shard_map/jvp(hm,hml->hl)/dot_general | solution.py:50
  892.2 292.0 %fusion.18 = f32[512,1,1024]{2,1,0:T(1,128)} fusion(f32[512,32,1]{1,2,0:T(1,128)S(1)} %copy.125, f32[512,32]{1,0:T(8,128)S(1)} %copy-done.52, f32[512,32]{1,0:T(8,128)S(1)} %copy-done.57), kind=kOutput, calls=%fused_computation.17 | convolution fusion | flops 150994944 | bytes 2293760 | tf_op jit(solution)/shard_map/jvp(hm,hml->hl)/dot_general | solution.py:49
  1204.5 39.5 fusion.124
  1244.0 39.4 fusion.136
  1285.2 53.4 %fusion.51 = f32[2,512,2048]{2,1,0:T(8,128)S(1)} fusion(bf16[2,1024,512]{2,1,0:T(8,128)(2,1)S(1)} %bitcast.257), kind=kOutput, calls=%fused_computation.63 | convolution fusion | flops 12914262016 | bytes 10485760 | tf_op jit(solution)/shard_map/jvp(slh,lf->shf)/dot_general | solution.py:65
  1338.6 44.9 fusion.59
  1397.7 49.4 %fusion.49 = f32[1024,2,512]{2,0,1:T(8,128)} fusion(f32[2,512,2048]{2,1,0:T(8,128)} %fusion.354), kind=kOutput, calls=%fused_computation.61 | convolution fusion | flops 12914262016 | bytes 12582912 | tf_op jit(solution)/shard_map/jvp(shf,lf->slh)/dot_general | solution.py:72
  1447.2 54.7 %multiply_convert_fusion.4 = (bf16[2,1024,512]{2,1,0:T(8,128)(2,1)S(1)}, f32[2,1024,512]{2,1,0:T(8,128)}, f32[2,1024,512]{2,1,0:T(8,128)}) fusion(bf16[2,1024,512]{2,1,0:T(8,128)(2,1)S(1)} %bitcast.259, f32[512]{0:T(512)S(1)} %copy-done.98, f32[512,1024,2]{0,1,2:T(8,128)S(1)} %copy-done.27, f32[512,1024,2]{0,1,2:T(8,128)S(1)} %copy-done.26, ...), kind=kOutput, calls=%fused_computation.148 | convolution fusion | flops 12990808064 | bytes 33556480 | tf_op jit(solution)/shard_map/jvp(shf,lf->slh)/dot_general | solution.py:71
  1511.5 192.0 %reduce-scatter.5.cloned.1.call-done = f32[1024,2048]{1,0:T(8,128)} async-done(((f32[2048,2048]{1,0:T(8,128)}), f32[1024,2048]{1,0:T(8,128)}) %reduce-scatter.5.cloned.1.call-update) | async-done | bytes 8388624 | tf_op jit(solution)/shard_map/reduce_scatter | solution.py:119
  1713.3 56.3 %all-gather.7.cloned.1.call-done = bf16[2048,1024]{1,0:T(8,128)(2,1)} async-done(((bf16[1024,1024]{1,0:T(8,128)(2,1)}), bf16[2048,1024]{1,0:T(8,128)(2,1)}) %all-gather.7.cloned.1.call-update) | async-done | bytes 4194320 | tf_op jit(solution)/shard_map/all_gather | solution.py:129
  1769.6 48.6 %multiply_convert_fusion = (bf16[2048,2048]{1,0:T(8,128)(2,1)}, f32[2048,2048]{1,0:T(8,128)}, f32[2048,2048]{1,0:T(8,128)}) fusion(bf16[2048,1024]{1,0:T(8,128)(2,1)} %all-gather.7.cloned.1.call-done, bf16[1024,2048]{1,0:T(8,128)(2,1)} %param.23), kind=kOutput, calls=%fused_computation.37 | convolution fusion | flops 8862564352 | bytes 50331648 | tf_op jit(solution)/shard_map/dot_general | solution.py:130
  1827.8 22.3 add_convert_fusion
  1878.4 84.8 %reduce-scatter.9.cloned.1.call-done = f32[1024,1024]{1,0:T(8,128)} async-done(((f32[2048,1024]{1,0:T(8,128)}), f32[1024,1024]{1,0:T(8,128)}) %reduce-scatter.9.cloned.1.call-update) | async-done | bytes 4194320 | tf_op jit(solution)/shard_map/reduce_scatter | solution.py:147
  1968.1 96.6 %reduce-scatter.7.cloned.1.call-done = f32[1024,1024]{1,0:T(8,128)} async-done(((f32[2048,1024]{1,0:T(8,128)}), f32[1024,1024]{1,0:T(8,128)}) %reduce-scatter.7.cloned.1.call-update) | async-done | bytes 4194320 | tf_op jit(solution)/shard_map/reduce_scatter | solution.py:133
  2109.2 75.2 %all-gather.11.cloned.1.call-done = bf16[2048,2048]{1,0:T(8,128)(2,1)} async-done(((bf16[1024,2048]{1,0:T(8,128)(2,1)}), bf16[2048,2048]{1,0:T(8,128)(2,1)}) %all-gather.11.cloned.1.call-update) | async-done | bytes 8388624 | tf_op jit(solution)/shard_map/all_gather | solution.py:158
  2202.4 57.4 %fusion.47 = f32[2,512,2048]{2,1,0:T(8,128)} fusion(f32[1024,2,512]{2,0,1:T(8,128)S(1)} %fusion.352), kind=kOutput, calls=%fused_computation.59 | convolution fusion | flops 12914262016 | bytes 12582912 | tf_op jit(solution)/shard_map/transpose(jvp(shf,lf->slh))/dot_general | solution.py:72
  2259.8 68.7 %multiply_reduce_fusion.4 = (f32[512,2048]{1,0:T(8,128)}, f32[512,2048]{1,0:T(8,128)}, f32[512,2048]{1,0:T(8,128)}, f32[512,2048]{1,0:T(8,128)}, f32[2,512,2048]{2,1,0:T(8,128)}) fusion(f32[2,512,2048]{2,1,0:T(8,128)} %copy-done.11, f32[2,512,2048]{2,1,0:T(8,128)} %fusion.59, f32[2,512,2048]{2,1,0:T(8,128)} %fusion.47, f32[1024,2,512]{2,0,1:T(8,128)S(1)} %fusion.97.clone.5), kind=kOutput, calls=%fused_computation.75 | convolution fusion | flops 12928942080 | bytes 54525952 | tf_op jit(solution)/shard_map/transpose(jvp(shf,lf->slh))/dot_general | solution.py:71
  2358.9 272.7 %fusion.159 = f32[2,512,32]{2,0,1:T(2,128)} fusion(f32[512,1024,2]{1,2,0:T(2,128)} %copy.111, f32[512,32]{1,0:T(8,128)S(1)} %copy-done.53, f32[512,32]{1,0:T(8,128)S(1)} %copy-done.58), kind=kOutput, calls=%fused_computation.188 | convolution fusion | flops 251658240 | bytes 4456448 | tf_op jit(solution)/shard_map/transpose(jvp(shm,hml->slh))/dot_general | solution.py:61
  2631.7 31.7 fusion.225
  2664.6 38.6 fusion.99
  2705.4 39.7 negate_bitcast_fusion.1
  2748.0 48.3 %fusion.45 = f32[2,512,1024]{1,2,0:T(8,128)S(1)} fusion(f32[2,512,2048]{2,1,0:T(8,128)} %fusion.350), kind=kOutput, calls=%fused_computation.57 | convolution fusion | flops 12914262016 | bytes 12582912 | tf_op jit(solution)/shard_map/transpose(jvp(slh,lf->shf))/dot_general | solution.py:65
  2796.4 44.7 fusion.96
  2852.7 380.0 %multiply_reduce_fusion.1 = (f32[512,32]{1,0:T(8,128)}, f32[512,32]{1,0:T(8,128)}) fusion(f32[512,32,1024]{2,1,0:T(8,128)} %fusion.225, f32[512,32]{1,0:T(8,128)S(1)} %copy-done.30, f32[512,1024]{1,0:T(8,128)} %copy-done.35, f32[512,32]{1,0:T(8,128)S(1)} %copy-done.44, f32[512,1024]{1,0:T(8,128)} %neg.90, f32[512,32]{1,0:T(8,128)S(1)} %copy-done.54, ...), kind=kOutput, calls=%fused_computation.3 | convolution fusion | flops 536936448 | bytes 76283904 | tf_op jit(solution)/shard_map/transpose(jvp(shm,hml->slh))/dot_general | solution.py:62
  3232.7 305.6 %multiply_bitcast_fusion.2 = (f32[1,2,512,32]{3,1,2,0:T(2,128)}, f32[2,512,32]{2,0,1:T(2,128)}, f32[1,2,512,32]{3,1,2,0:T(2,128)}, f32[2,512,32]{2,0,1:T(2,128)}...) fusion(f32[512,32]{1,0:T(8,128)S(1)} %copy-done.44, ...), kind=kOutput, calls=%fused_computation.209 | convolution fusion | flops 252182528 | bytes 5701632 | tf_op jit(solution)/shard_map/transpose(jvp(shm,hml->slh))/dot_general | solution.py:62
  3549.3 260.3 %fusion.4 = f32[512,1,32]{2,1,0:T(1,128)S(1)} fusion(f32[512,32]{1,0:T(8,128)} %copy.96, f32[512,32]{1,0:T(8,128)} %copy.95, f32[512,1024,1]{1,0,2:T(8,128)} %get-tuple-element.97), kind=kOutput, calls=%fused_computation.10 | convolution fusion | flops 150994944 | bytes 2293760 | tf_op jit(solution)/shard_map/transpose(jvp(hm,hml->hl))/dot_general | solution.py:50
  3809.6 297.9 %fusion.12 = f32[512,1,32]{2,1,0:T(1,128)S(1)} fusion(f32[512,32]{1,0:T(8,128)S(1)} %copy-done.55, f32[512,32]{1,0:T(8,128)S(1)} %copy-done.61, f32[512,1024,1]{1,0,2:T(8,128)S(1)} %bitcast.256), kind=kOutput, calls=%fused_computation.14 | convolution fusion | flops 150994944 | bytes 2293760 | tf_op jit(solution)/shard_map/transpose(jvp(hm,hml->hl))/dot_general | solution.py:49
  4119.2 35.3 all-reduce.11
  4161.1 38.6 all-reduce.10
  4205.6 286.5 %all-reduce.15.cloned.1.call-done = (f32[512,32]{0,1:T(8,128)}, f32[512,32]{0,1:T(8,128)}, f32[2,512,32]{2,1,0:T(8,128)}, f32[512,2048]{1,0:T(8,128)}, f32[1024,2048]{1,0:T(8,128)}, /*index=5*/f32[2048,1024]{1,0:T(8,128)}) async-done(((f32[512,32]{0,1:T(8,128)}, f32[512,32]{0,1:T(8,128)}, f32[2,512,32]{2,1,0:T(8,128)}, f32[512,2048]{1,0:T(8,128)}, f32[1024,2048]{1,0:T(8,128)}, ...) | async-done | bytes 21233680 | tf_op jit(solution)/shard_map/psum | solution.py:185
  (326 shorter events, 278.9 us)
Async XLA Ops:
  7.2 1496.0 %copy-start = (bf16[512,2048]{1,0:T(8,128)(2,1)S(1)}, bf16[512,2048]{1,0:T(8,128)(2,1)}, u32[]{:S(2)}) copy-start(bf16[512,2048]{1,0:T(8,128)(2,1)} %param.21) | copy-start | bytes 6291460
  7.3 1276.2 %all-gather.5.cloned.1.call-start = ((), (), s32[]{:S(2)}) async-start(), calls=%async_computation.4 | async-start | bytes 6291456 | tf_op jit(solution)/shard_map/all_gather | solution.py:99
  15.3 1688.1 %reduce-scatter.5.cloned.1.call-start = ((), (), s32[]{:S(2)}) async-start(), calls=%async_computation.5 | async-start | bytes 25165824 | tf_op jit(solution)/shard_map/reduce_scatter | solution.py:119
  15.5 1186.1 %copy-start.89 = (f32[512]{0:T(512)}, f32[512]{0:T(512)S(1)}, u32[]{:S(2)}) copy-start(f32[512]{0:T(512)S(1)} %get-tuple-element.141) | copy-start | bytes 6148
  21.0 277.1 %copy-start.29 = (f32[512,32]{1,0:T(8,128)}, f32[512,32]{1,0:T(8,128)S(1)}, u32[]{:S(2)}) copy-start(f32[512,32]{1,0:T(8,128)S(1)} %copy.98) | copy-start | bytes 196612
  21.4 276.8 %copy-start.18 = (f32[1,2,512,32]{3,1,2,0:T(2,128)}, f32[1,2,512,32]{3,1,2,0:T(2,128)S(1)}, u32[]{:S(2)}) copy-start(f32[1,2,512,32]{3,1,2,0:T(2,128)S(1)} %copy.138) | copy-start | bytes 393220
  21.6 276.6 %copy-start.20 = (f32[1,2,512,32]{3,1,2,0:T(2,128)}, f32[1,2,512,32]{3,1,2,0:T(2,128)S(1)}, u32[]{:S(2)}) copy-start(f32[1,2,512,32]{3,1,2,0:T(2,128)S(1)} %copy.139) | copy-start | bytes 393220
  23.3 274.9 %copy-start.31 = (f32[2,512,32]{2,0,1:T(2,128)}, f32[2,512,32]{2,0,1:T(2,128)S(1)}, u32[]{:S(2)}) copy-start(f32[2,512,32]{2,0,1:T(2,128)S(1)} %get-tuple-element.125) | copy-start | bytes 393220
  23.3 274.9 %copy-start.33 = (f32[2,512,32]{2,0,1:T(2,128)}, f32[2,512,32]{2,0,1:T(2,128)S(1)}, u32[]{:S(2)}) copy-start(f32[2,512,32]{2,0,1:T(2,128)S(1)} %get-tuple-element.126) | copy-start | bytes 393220
  298.2 292.2 %copy-start.66 = (f32[512,32,1]{0,1,2:T(8,128)S(1)}, f32[512,32,1]{0,1,2:T(8,128)}, u32[]{:S(2)}) copy-start(f32[512,32,1]{0,1,2:T(8,128)} %get-tuple-element.137) | copy-start | bytes 196612
  298.2 292.3 %copy-start.65 = (f32[512,32,1]{0,1,2:T(8,128)S(1)}, f32[512,32,1]{0,1,2:T(8,128)}, u32[]{:S(2)}) copy-start(f32[512,32,1]{0,1,2:T(8,128)} %get-tuple-element.138) | copy-start | bytes 196612
  590.7 301.5 %copy-start.52 = (f32[512,32]{1,0:T(8,128)S(1)}, f32[512,32]{1,0:T(8,128)}, u32[]{:S(2)}) copy-start(f32[512,32]{1,0:T(8,128)} %copy.96) | copy-start | bytes 196612
  590.7 301.5 %copy-start.57 = (f32[512,32]{1,0:T(8,128)S(1)}, f32[512,32]{1,0:T(8,128)}, u32[]{:S(2)}) copy-start(f32[512,32]{1,0:T(8,128)} %copy.95) | copy-start | bytes 196612
  1511.4 258.1 %all-gather.7.cloned.1.call-start = ((), (), s32[]{:S(2)}) async-start(), calls=%async_computation.6 | async-start | bytes 6291456 | tf_op jit(solution)/shard_map/all_gather | solution.py:129
  1712.7 115.1 %all-gather.9.cloned.1.call-start = ((), (), s32[]{:S(2)}) async-start(), calls=%async_computation.8 | async-start | bytes 6291456 | tf_op jit(solution)/shard_map/all_gather | solution.py:140
  1713.3 250.0 %reduce-scatter.9.cloned.1.call-start = ((), (), s32[]{:S(2)}) async-start(), calls=%async_computation.9 | async-start | bytes 12582912 | tf_op jit(solution)/shard_map/reduce_scatter | solution.py:147
  1863.9 200.8 %reduce-scatter.7.cloned.1.call-start = ((), (), s32[]{:S(2)}) async-start(), calls=%async_computation.7 | async-start | bytes 12582912 | tf_op jit(solution)/shard_map/reduce_scatter | solution.py:133
  1878.4 306.0 %all-gather.11.cloned.1.call-start = ((), (), s32[]{:S(2)}) async-start(), calls=%async_computation.10 | async-start | bytes 12582912 | tf_op jit(solution)/shard_map/all_gather | solution.py:158
  2080.2 2074.3 %reduce-scatter.11.cloned.1.call-start = ((), (), s32[]{:S(2)}) async-start(), calls=%async_computation.11 | async-start | bytes 6291456 | tf_op jit(solution)/shard_map/reduce_scatter | solution.py:169
  2845.1 1647.0 %all-reduce.15.cloned.1.call-start = ((), (), s32[]{:S(2)}) async-start(), calls=%async_computation.12 | async-start | bytes 43253760 | tf_op jit(solution)/shard_map/psum | solution.py:185
  2852.7 380.0 %copy-start.28 = (f32[512,1024,2]{1,2,0:T(2,128)S(1)}, f32[512,1024,2]{1,2,0:T(2,128)}, u32[]{:S(2)}) copy-start(f32[512,1024,2]{1,2,0:T(2,128)} %copy.110) | copy-start | bytes 12582916
  2852.7 380.0 %copy-start.60 = (f32[512,32]{1,0:T(8,128)S(1)}, f32[512,32]{1,0:T(8,128)}, u32[]{:S(2)}) copy-start(f32[512,32]{1,0:T(8,128)} %copy.95) | copy-start | bytes 196612
  2852.7 380.0 %copy-start.102 = (f32[2,512,32]{2,0,1:T(2,128)S(1)}, f32[2,512,32]{2,0,1:T(2,128)}, u32[]{:S(2)}) copy-start(f32[2,512,32]{2,0,1:T(2,128)} %fusion.159) | copy-start | bytes 393220
  3232.7 311.9 %copy-start.19 = (f32[1,2,512,32]{3,1,2,0:T(2,128)S(1)}, f32[1,2,512,32]{3,1,2,0:T(2,128)}, u32[]{:S(2)}) copy-start(f32[1,2,512,32]{3,1,2,0:T(2,128)} %copy-done.18) | copy-start | bytes 393220
  3232.7 311.9 %copy-start.21 = (f32[1,2,512,32]{3,1,2,0:T(2,128)S(1)}, f32[1,2,512,32]{3,1,2,0:T(2,128)}, u32[]{:S(2)}) copy-start(f32[1,2,512,32]{3,1,2,0:T(2,128)} %copy-done.20) | copy-start | bytes 393220
  3549.3 560.0 %slice-start.4 = ((s8[8388608]{0:T(1024)(128)(4,1)}), s8[4194304]{0:T(1024)(128)(4,1)S(1)}, s32[]{:S(2)}) async-start(s8[8388608]{0:T(1024)(128)(4,1)} %bitcast.266), calls=%async_computation.17 | async-start | bytes 8388608
  3809.6 298.9 %copy-start.46 = (f32[512,32]{0,1:T(8,128)S(1)}, f32[512,32]{0,1:T(8,128)}, u32[]{:S(2)}) copy-start(f32[512,32]{0,1:T(8,128)} %copy-done.45) | copy-start | bytes 196612
  3809.6 298.9 %copy-start.48 = (f32[512,32]{0,1:T(8,128)S(1)}, f32[512,32]{0,1:T(8,128)}, u32[]{:S(2)}) copy-start(f32[512,32]{0,1:T(8,128)} %copy-done.47) | copy-start | bytes 196612
  3809.6 298.9 %copy-start.50 = (f32[512,32]{0,1:T(8,128)S(1)}, f32[512,32]{0,1:T(8,128)}, u32[]{:S(2)}) copy-start(f32[512,32]{0,1:T(8,128)} %copy-done.49) | copy-start | bytes 196612
  3809.6 298.9 %copy-start.88 = (f32[512]{0:T(512)S(1)}, f32[512]{0:T(512)}, u32[]{:S(2)}) copy-start(f32[512]{0:T(512)} %copy-done.87) | copy-start | bytes 6148
  3809.6 299.6 %slice-start.5 = ((s8[8388608]{0:T(1024)(128)(4,1)}), s8[4194304]{0:T(1024)(128)(4,1)S(1)}, s32[]{:S(2)}) async-start(s8[8388608]{0:T(1024)(128)(4,1)} %bitcast.266), calls=%async_computation.18 | async-start | bytes 8388608
  3809.6 299.6 %copy-start.101 = (bf16[2,1024,512]{2,1,0:T(8,128)(2,1)S(1)}, bf16[2,1024,512]{2,1,0:T(8,128)(2,1)}, u32[]{:S(2)}) copy-start(bf16[2,1024,512]{2,1,0:T(8,128)(2,1)} %copy-done.100) | copy-start | bytes 6291460
  (86 other events, 5455.8 us)
Sparse Core Ops, SparseCore 0:
  15.5 59.4 all-gather.4
  1511.6 191.8 reduce-scatter.4
  1712.8 56.7 all-gather.6
  1771.1 56.7 all-gather.8
  1864.0 99.2 reduce-scatter.8
  1965.4 99.2 reduce-scatter.6
  2080.4 103.9 all-gather.10
  2845.2 54.2 reduce-scatter.10
  4115.7 376.4 all-reduce.14
where the time goes:
time: 4530 us; the launch traced here: 4520 us
  matrix products  3450 us (76%)
  waiting for transfers between devices  802 us (18%)
  other arithmetic  108 us (2%)
  blocking collectives  74 us (2%)
  local copies, waits for them, and re-layouts  72 us (2%)
    dot_general x3, matrix products, mixer_local(): jnp.einsum('shm,hml->slh', wimag, sin_pow, precision=MEDIUM)  960 us
    dot_general x3, matrix products, mixer_local(): jnp.einsum('shm,hml->slh', wreal, cos_pow, precision=MEDIUM)  597 us
    dot_general x2, matrix products, mixer_local(): jnp.einsum('hm,hml->hl', readout[0], cos_pow, precision=MEDIUM)  590 us
    dot_general x2, matrix products, mixer_local(): jnp.einsum('hm,hml->hl', readout[1], sin_pow, precision=MEDIUM)  562 us
    psum x1, waiting for transfers between devices, local(): lax.psum((grad_glu, grad_ffn_in, grad_ffn_out, grad_step, grad_decay, gra...  287 us
    reduce_scatter x1, waiting for transfers between devices, local(): lax.psum_scatter(jnp.dot(glu_in, glu_weight, preferred_element_type=jnp.f...  192 us
    dot_general x2, matrix products, mixer_local(): jnp.einsum('shf,lf->slh', out_real, cos_table, precision=MEDIUM)  123 us
    dot_general x2, matrix products, mixer_local(): jnp.einsum('shf,lf->slh', out_imag, sin_table, precision=MEDIUM)  107 us
  transfers between devices with their start and end apart: 9, of which 7 were waited for; matrix products, arithmetic and copies ran while one was open for 59% of the time, Pallas kernels for 0%

commit v1 on v0

v1 whole, which is shorter than its diff:
```python
import functools
import math

import jax
import jax.numpy as jnp
import numpy as np
from jax import lax
from jax.experimental import pallas as pl
from jax.experimental.pallas import tpu as pltpu
from jax.sharding import PartitionSpec as P

SEQ_LEN = 1024
EPSILON = 1e-05
LANES = 128
F32 = jnp.float32
BF16 = jnp.bfloat16
VMEM_BYTES = 56 * 1024 * 1024


def cost(microseconds):
    return pl.CostEstimate(flops=int(microseconds * 9e8), bytes_accessed=0, transcendentals=0)


def split_low(v):
    high = v.astype(BF16)
    return high, (v - high.astype(F32)).astype(BF16)


def dot(a, b, dims=((1,), (0,))):
    return lax.dot_general(a, b, (dims, ((), ())), preferred_element_type=F32)


def dot_split(a, b, dims=((1,), (0,))):
    total = dot(a[0], b[0], dims)
    if a[1] is not None:
        total += dot(a[1], b[0], dims)
    if b[1] is not None:
        total += dot(a[0], b[1], dims)
    return total


def gelu_pair(u):
    z = jnp.abs(u) * (1.0 / math.sqrt(2.0))
    t = 1.0 / (1.0 + 0.3275911 * z)
    poly = t * (
        0.5 * 0.254829592
        + t
        * (
            0.5 * -0.284496736
            + t * (0.5 * 1.421413741 + t * (0.5 * -1.453152027 + t * (0.5 * 1.061405429)))
        )
    )
    bell = jnp.exp(-0.5 * u * u)
    tail = poly * bell
    cdf = jnp.where(u >= 0.0, 1.0 - tail, tail)
    return u * cdf, cdf + u * bell * (1.0 / math.sqrt(2.0 * math.pi))


def norm_parts(values):
    center = values - jnp.mean(values, axis=-1, keepdims=True)
    spread = jnp.mean(center * center, axis=-1, keepdims=True)
    inv = lax.rsqrt(spread + EPSILON)
    return center * inv, inv


def norm_back(normal, inv, gain, grad):
    scaled = grad * gain
    mean_grad = jnp.mean(scaled, axis=-1, keepdims=True)
    mean_dot = jnp.mean(scaled * normal, axis=-1, keepdims=True)
    return inv * (scaled - mean_grad - normal * mean_dot)


def cmul(a, b):
    return a[0] * b[0] - a[1] * b[1], a[0] * b[1] + a[1] * b[0]


def mode_powers(lam):
    squares = [lam]
    for _ in range(9):
        squares.append(cmul(squares[-1], squares[-1]))
    p1, p2, p4 = squares[7], squares[8], squares[9]
    p3 = cmul(p1, p2)
    return squares, [None, p1, p2, p3, p4, cmul(p4, p1), cmul(p4, p2), cmul(p4, p3)]


def row_of(pair, g):
    return pair[0][g : g + 1, :], pair[1][g : g + 1, :]


def spread_rows(row):
    return jnp.broadcast_to(row, (8, LANES))


def power_table(squares, g):
    index = lax.broadcasted_iota(jnp.int32, (8, LANES), 0)
    one = (jnp.ones((8, LANES), F32), jnp.zeros((8, LANES), F32))
    table = one
    for bit in range(3):
        row = row_of(squares[bit], g)
        picked = (index >> bit) & 1 == 1
        factor = (jnp.where(picked, spread_rows(row[0]), 1.0), jnp.where(picked, spread_rows(row[1]), 0.0))
        table = factor if bit == 0 else cmul(table, factor)
    tables = [table]
    for bit in range(3, 7):
        row = row_of(squares[bit], g)
        factor = (spread_rows(row[0]), spread_rows(row[1]))
        tables = tables + [cmul(t, factor) for t in tables]
    return tables


def stack_table(tables, part):
    return jnp.concatenate([t[part] for t in tables], axis=0)


def lane_masks():
    channel = lax.broadcasted_iota(jnp.int32, (8, LANES), 0)
    owner = lax.broadcasted_iota(jnp.int32, (8, LANES), 1) >> 5
    return [channel == owner, channel == owner + 4]


def synth_kernel(lr, li, kr, ki, wr, wi, k_ref, st_ref):
    lam = (lr[...], li[...])
    squares, far = mode_powers(lam)
    masks = lane_masks()
    coefs = []
    for base in ((kr[...], ki[...]), (wr[...], wi[...])):
        coefs.append([base if p is None else cmul(base, p) for p in far])
    outs = []
    for pair in range(lr.shape[0] // 2):
        columns, left = [], []
        for part in range(2):
            g = 2 * pair + part
            tables = power_table(squares, g)
            columns += [stack_table(tables, 0), stack_table(tables, 1)]
            real, imag = [], []
            for source in coefs:
                for value in source:
                    row = row_of(value, g)
                    real.append(jnp.where(masks[part], spread_rows(row[0]), 0.0))
                    imag.append(jnp.where(masks[part], spread_rows(-row[1]), 0.0))
            left += [jnp.concatenate(real, axis=0), jnp.concatenate(imag, axis=0)]
        right = split_low(jnp.concatenate(columns, axis=1))
        rows = split_low(jnp.concatenate(left, axis=1))
        outs.append(dot_split(rows, right, ((1,), (1,))))
    for twin in range(len(outs) // 2):
        first, second = outs[2 * twin], outs[2 * twin + 1]
        for a in range(8):
            lanes = slice(a * LANES, (a + 1) * LANES)
            both = jnp.concatenate([first[a * 8 : a * 8 + 8], second[a * 8 : a * 8 + 8]], axis=0)
            k_ref[twin * 16 : twin * 16 + 16, lanes] = both
            at = 64 + a * 8
            st_ref[twin * 16 : twin * 16 + 16, lanes] = jnp.concatenate(
                [first[at : at + 8], second[at : at + 8]], axis=0
            )


def synthesize(lam, kernel_coef, state_coef):
    groups = lam[0].shape[0]
    channels = groups * 4
    spec = pl.BlockSpec((8, LANES), lambda i: (i, 0))
    out = pl.BlockSpec((32, SEQ_LEN), lambda i: (i, 0))
    return pl.pallas_call(
        synth_kernel,
        grid=(groups // 8,),
        in_specs=[spec] * 6,
        out_specs=[out, out],
        out_shape=[
            jax.ShapeDtypeStruct((channels, SEQ_LEN), F32),
            jax.ShapeDtypeStruct((channels, SEQ_LEN), F32),
        ],
        compiler_params=pltpu.CompilerParams(vmem_limit_bytes=VMEM_BYTES),
        cost_estimate=cost(20),
        name="synth",
    )(*lam, *kernel_coef, *state_coef)


def moments_kernel(lr, li, dk_ref, dy_ref, *outs):
    lam = (lr[...], li[...])
    squares, far = mode_powers(lam)
    masks = lane_masks()
    index = lax.broadcasted_iota(jnp.int32, (8, LANES), 0).astype(F32)
    results = [[] for _ in outs]
    blocks = []
    for twin in range(lr.shape[0] // 4):
        per_source = []
        for ref in (dk_ref, dy_ref):
            per_source.append(ref[twin * 16 : twin * 16 + 16, :].astype(F32))
        for half in range(2):
            rows = []
            for value in per_source:
                own = value[half * 8 : half * 8 + 8]
                rows += [own[:, a * LANES : (a + 1) * LANES] for a in range(8)]
            blocks.append(jnp.concatenate(rows, axis=0).astype(BF16))
    for pair, left in enumerate(blocks):
        plain, weighted = [], []
        for part in range(2):
            tables = power_table(squares, 2 * pair + part)
            for which in range(2):
                plain.append(stack_table(tables, which).astype(BF16))
                weighted.append(
                    jnp.concatenate([t[which] * (index + 8.0 * j) for j, t in enumerate(tables)], axis=0).astype(BF16)
                )
        right = jnp.concatenate(plain + weighted, axis=1)
        sums = jnp.dot(left, right, preferred_element_type=F32)
        for part in range(2):
            g = 2 * pair + part
            for source in range(2):
                low, high = None, None
                for a in range(8):
                    at = source * 64 + a * 8
                    piece = [
                        sums[at : at + 8, (base + 2 * part + which) * LANES : (base + 2 * part + which + 1) * LANES]
                        for base in (0, 4)
                        for which in range(2)
                    ]
                    u = (piece[0], piece[1])
                    v = (piece[2] + (128.0 * a) * piece[0], piece[3] + (128.0 * a) * piece[1])
                    if far[a] is not None:
                        row = row_of(far[a], g)
                        factor = (spread_rows(row[0]), spread_rows(row[1]))
                        u, v = cmul(u, factor), cmul(v, factor)
                    low = u if low is None else (low[0] + u[0], low[1] + u[1])
                    high = v if high is None else (high[0] + v[0], high[1] + v[1])
                for slot, value in enumerate(low + high):
                    picked = jnp.where(masks[part], value, 0.0)
                    results[source * 4 + slot].append(jnp.sum(picked, axis=0, keepdims=True))
    for ref, rows in zip(outs, results):
        ref[...] = jnp.concatenate(rows, axis=0)


def moments(lam, dk, dy):
    groups = lam[0].shape[0]
    spec = pl.BlockSpec((8, LANES), lambda i: (i, 0))
    wide = pl.BlockSpec((32, SEQ_LEN), lambda i: (i, 0))
    return pl.pallas_call(
        moments_kernel,
        grid=(groups // 8,),
        in_specs=[spec, spec, wide, wide],
        out_specs=[spec] * 8,
        out_shape=[jax.ShapeDtypeStruct((groups, LANES), F32)] * 8,
        compiler_params=pltpu.CompilerParams(vmem_limit_bytes=VMEM_BYTES),
        cost_estimate=cost(25),
        name="moments",
    )(*lam, dk, dy)


@functools.lru_cache(maxsize=1)
def transform_tables():
    times = np.arange(SEQ_LEN, dtype=np.int64)
    odd = 2 * np.arange(SEQ_LEN, dtype=np.int64) + 1
    theta = (times[:, None] * odd[None, :] % (4 * SEQ_LEN)) * (math.pi / (2 * SEQ_LEN))
    both = np.concatenate([np.cos(theta), np.sin(theta)], axis=1)
    high = both.astype(jnp.bfloat16)
    low = (both - high.astype(np.float64)).astype(jnp.bfloat16)
    turned = lambda v: np.ascontiguousarray(v.T)
    return high, low, turned(high), turned(low)


def conv_forward_kernel(x_ref, k_ref, st_ref, skip_ref, forth, forth_low, back, back_low, mixed_ref, slope_ref, xf_ref, kf_ref):
    half = SEQ_LEN
    x = x_ref[...]
    table = (forth[...], forth_low[...])
    xf = dot_split((x, None), table)
    kf = dot_split(split_low(k_ref[...]), table)
    xf_ref[...] = xf.astype(BF16)
    kf_ref[...] = kf.astype(BF16)
    xr, xs, kr, ks = xf[:, :half], xf[:, half:], kf[:, :half], kf[:, half:]
    conv = dot_split(split_low(xr * kr - xs * ks), (back[:half, :], back_low[:half, :]))
    conv += dot_split(split_low(xr * ks + xs * kr), (back[half:, :], back_low[half:, :]))
    value = conv * (1.0 / half) + st_ref[...] + skip_ref[...] * x.astype(F32)
    mixed, slope = gelu_pair(value)
    mixed_ref[...] = mixed.astype(BF16)
    slope_ref[...] = slope


def whole_spec(v):
    return pl.BlockSpec(v.shape, lambda i: (0, 0), pipeline_mode=pl.Buffered(1))


def conv_forward(xt, kernel, state_term, skip):
    channels = xt.shape[0]
    block = min(256, channels)
    tables = [jnp.asarray(v) for v in transform_tables()]
    wide = pl.BlockSpec((block, SEQ_LEN), lambda i: (i, 0))
    double = pl.BlockSpec((block, 2 * SEQ_LEN), lambda i: (i, 0))
    return pl.pallas_call(
        conv_forward_kernel,
        grid=(channels // block,),
        in_specs=[wide, wide, wide, pl.BlockSpec((block, 1), lambda i: (i, 0))] + [whole_spec(v) for v in tables],
        out_specs=[wide, wide, double, double],
        out_shape=[
            jax.ShapeDtypeStruct((channels, SEQ_LEN), BF16),
            jax.ShapeDtypeStruct((channels, SEQ_LEN), F32),
            jax.ShapeDtypeStruct((channels, 2 * SEQ_LEN), BF16),
            jax.ShapeDtypeStruct((channels, 2 * SEQ_LEN), BF16),
        ],
        compiler_params=pltpu.CompilerParams(vmem_limit_bytes=VMEM_BYTES),
        cost_estimate=cost(40),
        name="conv_forward",
    )(xt, kernel, state_term, skip, *tables)


def conv_backward_kernel(g_ref, slope_ref, x_ref, xf_ref, kf_ref, skip_ref, forth, back, dx_ref, dk_ref, dy_ref, dskip_ref):
    half = SEQ_LEN
    x = x_ref[...].astype(F32)
    dy = g_ref[...] * slope_ref[...]
    dskip_ref[...] = jnp.sum(dy * x, axis=1, keepdims=True)
    dy_low = dy.astype(BF16)
    dy_ref[...] = dy_low
    df = jnp.dot(dy_low, forth[...], preferred_element_type=F32) * (1.0 / half)
    dr, ds = df[:, :half], df[:, half:]
    for other, out, extra in ((kf_ref, dx_ref, skip_ref[...] * dy), (xf_ref, dk_ref, None)):
        r, s = other[:, :half].astype(F32), other[:, half:].astype(F32)
        real = (dr * r + ds * s).astype(BF16)
        imag = (ds * r - dr * s).astype(BF16)
        total = jnp.dot(real, back[:half, :], preferred_element_type=F32)
        total += jnp.dot(imag, back[half:, :], preferred_element_type=F32)
        if extra is not None:
            total += extra
        out[...] = total.astype(BF16)


def conv_backward(grad, slope, xt, xf, kf, skip):
    channels = xt.shape[0]
    block = min(256, channels)
    forth, _, back, _ = [jnp.asarray(v) for v in transform_tables()]
    wide = pl.BlockSpec((block, SEQ_LEN), lambda i: (i, 0))
    double = pl.BlockSpec((block, 2 * SEQ_LEN), lambda i: (i, 0))
    thin = pl.BlockSpec((block, 1), lambda i: (i, 0))
    low = jax.ShapeDtypeStruct((channels, SEQ_LEN), BF16)
    return pl.pallas_call(
        conv_backward_kernel,
        grid=(channels // block,),
        in_specs=[
            wide,
            wide,
            wide,
            double,
            double,
            thin,
            whole_spec(forth),
            whole_spec(back),
        ],
        out_specs=[wide, wide, wide, thin],
        out_shape=[low, low, low, jax.ShapeDtypeStruct((channels, 1), F32)],
        compiler_params=pltpu.CompilerParams(vmem_limit_bytes=VMEM_BYTES),
        cost_estimate=cost(22),
        name="conv_backward",
    )(grad, slope, xt, xf, kf, skip, forth, back)


def ffn_kernel(order, x_ref, xt_ref, c_ref, win_ref, wout_ref, branch_ref, dx_ref, dwin_ref, dwout_ref, act_ref, dh_ref):
    step = pl.program_id(0)
    rows = x_ref.shape[0]
    chunk = min(256, rows)

    @pl.when(step == 0)
    def _():
        branch_ref[...] = jnp.zeros_like(branch_ref)
        dx_ref[...] = jnp.zeros_like(dx_ref)

    win, wout = win_ref[...], wout_ref[...]
    for start in range(0, rows, chunk):
        own = slice(start, start + chunk)
        hidden = jnp.dot(x_ref[own, :], win, preferred_element_type=F32)
        d_act = lax.dot_general(c_ref[own, :], wout, (((1,), (1,)), ((), ())), preferred_element_type=F32)
        act, slope = gelu_pair(hidden)
        act = act.astype(BF16)
        dh = (d_act * slope).astype(BF16)
        act_ref[own, :] = act
        dh_ref[own, :] = dh
        branch_ref[own, :] += jnp.dot(act, wout, preferred_element_type=F32)
        dx_ref[own, :] += lax.dot_general(dh, win, (((1,), (1,)), ((), ())), preferred_element_type=F32)
    dwin_ref[0] = jnp.dot(xt_ref[...], dh_ref[...], preferred_element_type=F32).astype(BF16)
    dwout_ref[0] = lax.dot_general(
        act_ref[...], c_ref[...], (((0,), (0,)), ((), ())), preferred_element_type=F32
    ).astype(BF16)


def ffn(x, xt, c, win, wout, order):
    rows, width = x.shape
    hidden = win.shape[1]
    pieces = order.shape[0]
    block = hidden // pieces
    whole = lambda shape: pl.BlockSpec(shape, lambda i, order: (0, 0))
    return pl.pallas_call(
        ffn_kernel,
        grid_spec=pltpu.PrefetchScalarGridSpec(
            num_scalar_prefetch=1,
            grid=(pieces,),
            in_specs=[
                whole((rows, width)),
                whole((width, rows)),
                whole((rows, width)),
                pl.BlockSpec((width, block), lambda i, order: (0, order[i])),
                pl.BlockSpec((block, width), lambda i, order: (order[i], 0)),
            ],
            out_specs=[
                whole((rows, width)),
                whole((rows, width)),
                pl.BlockSpec((1, width, block), lambda i, order: (i, 0, 0)),
                pl.BlockSpec((1, block, width), lambda i, order: (i, 0, 0)),
            ],
            scratch_shapes=[pltpu.VMEM((rows, block), BF16), pltpu.VMEM((rows, block), BF16)],
        ),
        out_shape=[
            jax.ShapeDtypeStruct((rows, width), F32),
            jax.ShapeDtypeStruct((rows, width), F32),
            jax.ShapeDtypeStruct((pieces, width, block), BF16),
            jax.ShapeDtypeStruct((pieces, block, width), BF16),
        ],
        compiler_params=pltpu.CompilerParams(vmem_limit_bytes=VMEM_BYTES),
        cost_estimate=cost(36 * hidden / 2048),
        name="ffn",
    )(order, x, xt, c, win, wout)


class Pairs:
    def __init__(self, dp_size):
        self.dp_size = dp_size
        self.dp = lax.axis_index("dp")
        self.mp = lax.axis_index("mp")
        self.depth = dp_size // 4
        self.z = self.dp >> 2
        own = self.dp & 3
        self.order = jnp.stack([own, own ^ 2, own ^ 1, own ^ 3])

    def swap_y(self, v):
        return lax.ppermute(v, "mp", [(0, 1), (1, 0)])

    def swap_core(self, v):
        return lax.ppermute(v, "dp", [(i, i ^ 1) for i in range(self.dp_size)])

    def swap_x(self, v):
        return lax.ppermute(v, "dp", [(i, i ^ 2) for i in range(self.dp_size)])

    def shift_z(self, v, by):
        return lax.ppermute(v, "dp", [(i, (i + 4 * by) % self.dp_size) for i in range(self.dp_size)])

    def by_half(self, own, other, axis=0):
        first = jnp.where(self.mp == 0, own, other)
        second = jnp.where(self.mp == 0, other, own)
        return jnp.concatenate([first, second], axis=axis)

    def partner_shard(self, shard, axis):
        piece = shard.shape[axis] // 4
        mine = lax.dynamic_slice_in_dim(shard, self.order[0] * piece, piece, axis)
        first = self.swap_y(mine)
        second = self.swap_x(first)
        return [first, second, self.swap_core(first), self.swap_core(second)]

    def reduce(self, own, other):
        add = lambda a, b: (a.astype(F32) + b.astype(F32)).astype(BF16)
        other_two = add(other[:2], self.swap_core(other[2:]))
        own_two = add(own[:2], self.swap_core(own[2:]))
        own_two = add(own_two, self.swap_y(other_two))
        first = add(own_two[0], self.swap_x(own_two[1]))
        depth = self.depth
        parts = first.reshape((depth, first.shape[0] // depth) + first.shape[1:])
        total = lax.dynamic_index_in_dim(parts, self.z, 0, False).astype(F32)
        for by in range(1, depth):
            part = lax.dynamic_index_in_dim(parts, (self.z + by) % depth, 0, False)
            total = total + self.shift_z(part, by).astype(F32)
        total = total.astype(BF16)
        whole = jnp.zeros_like(parts)
        whole = lax.dynamic_update_index_in_dim(whole, total, self.z, 0)
        for by in range(1, depth):
            got = self.shift_z(total, by)
            whole = lax.dynamic_update_index_in_dim(whole, got, (self.z - by) % depth, 0)
        first = whole.reshape(first.shape)
        second = self.swap_x(first)
        return [first, second, self.swap_core(first), self.swap_core(second)]

    def place(self, pieces, axis):
        shape = list(pieces[0].shape)
        width = shape[axis]
        shape[axis] = 4 * width
        out = jnp.zeros(shape, F32)
        for at, piece in enumerate(pieces):
            out = lax.dynamic_update_slice_in_dim(out, piece.astype(F32), self.order[at] * width, axis)
        return out

    def sum_small(self, v):
        half = v.shape[0] // 2
        core = self.dp & 1
        mine = lax.dynamic_slice_in_dim(v, core * half, half, 0)
        mine = mine + self.swap_core(lax.dynamic_slice_in_dim(v, (1 - core) * half, half, 0))
        bit = 2
        while bit < self.dp_size:
            mine = mine + lax.ppermute(mine, "dp", [(i, i ^ bit) for i in range(self.dp_size)])
            bit *= 2
        other = self.swap_core(mine)
        first = jnp.where(core == 0, mine, other)
        second = jnp.where(core == 0, other, mine)
        return jnp.concatenate([first, second], axis=0)


def mode_terms(log_step, decay_rate, frequency, readout, state):
    rows = lambda v: v.reshape(-1, LANES)
    step = jnp.exp(log_step)[:, None]
    rate, turn = decay_rate * step, frequency * step
    decay = jnp.exp(-rate)
    lam = (rows(decay * jnp.cos(turn)), rows(decay * jnp.sin(turn)))
    out = (rows(readout[0]), rows(readout[1]))
    prior = (rows(state[0]), rows(state[1]))
    two_step = rows(jnp.broadcast_to(2.0 * step, decay_rate.shape))
    kernel_coef = (two_step * out[0], two_step * out[1])
    carried = cmul(lam, out)
    state_coef = cmul(carried, prior)
    return lam, out, prior, two_step, kernel_coef, carried, (2.0 * state_coef[0], 2.0 * state_coef[1])


def mode_grads(terms, sums, log_step, decay_rate, frequency):
    lam, out, prior, two_step, kernel_coef, carried, state_coef = terms
    kg, kh, sg, sh = sums[0:2], sums[2:4], sums[4:6], sums[6:8]
    through = cmul(lam, prior)
    readout_k = (two_step * kg[0], two_step * kg[1])
    readout_s = cmul(sg, through)
    grad_out = (readout_k[0] + 2.0 * readout_s[0], -(readout_k[1] + 2.0 * readout_s[1]))
    grad_prior = cmul(sg, carried)
    grad_prior = (2.0 * grad_prior[0], -2.0 * grad_prior[1])
    of_kernel = cmul(kernel_coef, kh)
    of_state = cmul(state_coef, (sg[0] + sh[0], sg[1] + sh[1]))
    grad_rate = -(of_kernel[0] + of_state[0])
    grad_turn = -(of_kernel[1] + of_state[1])
    channels = log_step.shape[0]
    back = lambda v: v.reshape(channels, -1)
    step = jnp.exp(log_step)[:, None]
    grad_rate, grad_turn = back(grad_rate), back(grad_turn)
    direct = back(cmul(kernel_coef, kg)[0])
    grad_step = jnp.sum(direct + step * (decay_rate * grad_rate + frequency * grad_turn), axis=1)
    grad_out = jnp.stack([back(grad_out[0]), back(grad_out[1])])
    grad_prior = jnp.stack([back(grad_prior[0]), back(grad_prior[1])])
    return grad_step, step * grad_rate, step * grad_turn, grad_out, grad_prior


def local(
    tokens,
    premix_gain,
    log_step,
    decay_rate,
    frequency,
    readout,
    skip_gain,
    prior_state,
    glu_weight,
    preffn_gain,
    ffn_in,
    ffn_out,
    cotangent,
):
    rows, width = tokens.shape
    mp_size, dp_size = lax.axis_size("mp"), lax.axis_size("dp")
    shard = log_step.shape[0]
    modes = decay_rate.shape[1]
    split = SEQ_LEN // rows
    channels = width // split
    mp = lax.axis_index("mp")
    paired = mp_size == 2 and dp_size == 16 and split == 1
    pairs = Pairs(dp_size) if paired else None

    if paired:
        take = lambda at: lax.dynamic_index_in_dim(prior_state, at, 1, False)
        common = jnp.stack([decay_rate, frequency, readout[0], readout[1]])
        vectors = jnp.stack([log_step, skip_gain]).reshape(1, -1, modes)
        flat = lambda *parts: jnp.concatenate([p.reshape(-1, modes) for p in parts], axis=0)
        got = pairs.swap_y(flat(common, vectors, take(1 - mp)))
        own = flat(common, vectors, take(mp))
        cut = 4 * shard + 2 * shard // modes

        def unpack(v):
            body = jnp.concatenate([v[: 4 * shard], v[cut:]]).reshape(6, shard, modes)
            return body, v[4 * shard : cut].reshape(2, shard)

        own_body, own_vec = unpack(own)
        got_body, got_vec = unpack(got)
        body = pairs.by_half(own_body, got_body, axis=1)
        vec = pairs.by_half(own_vec, got_vec, axis=1)
        my_decay, my_freq, my_readout, my_state = body[0], body[1], body[2:4], body[4:6]
        my_step, my_skip = vec[0], vec[1]
    else:
        gather = lambda v, axis: lax.all_gather(v, "mp", axis=axis, tiled=True)
        slot = (mp % split) * channels
        pick = lambda v, axis: lax.dynamic_slice_in_dim(gather(v, axis), slot, channels, axis)
        my_decay, my_freq = pick(decay_rate, 0), pick(frequency, 0)
        my_readout, my_step, my_skip = pick(readout, 1), pick(log_step, 0), pick(skip_gain, 0)
        my_state = lax.dynamic_index_in_dim(pick(prior_state, 2), mp // split, 1, False)

    def to_channels(v):
        if split == 1:
            return v
        every = lax.all_gather(v, "mp", axis=0, tiled=True)
        return lax.dynamic_slice(every, ((mp // split) * SEQ_LEN, (mp % split) * channels), (SEQ_LEN, channels))

    def to_rows(v):
        if split == 1:
            return v
        every = jnp.zeros((rows * mp_size, width), v.dtype)
        every = lax.dynamic_update_slice(every, v, ((mp // split) * SEQ_LEN, (mp % split) * channels))
        return lax.psum_scatter(every, "mp", scatter_dimension=0, tiled=True)

    if paired:
        glu_pieces = pairs.partner_shard(glu_weight, 0)
        in_pieces = pairs.partner_shard(ffn_in, 1)
        out_pieces = pairs.partner_shard(ffn_out, 0)
        quarter = shard // 4
        glu_full = jnp.zeros((width, 2 * width), BF16)
        glu_full = lax.dynamic_update_slice_in_dim(glu_full, glu_weight, mp * shard, 0)
        for at, piece in enumerate(glu_pieces):
            glu_full = lax.dynamic_update_slice_in_dim(
                glu_full, piece, (1 - mp) * shard + pairs.order[at] * quarter, 0
            )
    else:
        glu_full = lax.all_gather(glu_weight, "mp", axis=0, tiled=True)

    tok = tokens.astype(F32)
    normal, inv = norm_parts(tok)
    mixin = (normal * premix_gain).astype(BF16)
    mix_t = to_channels(mixin).T
    terms = mode_terms(my_step, my_decay, my_freq, my_readout, my_state)
    lam = terms[0]
    kernel, state_term = synthesize(lam, terms[4], terms[6])
    skip_column = my_skip[:, None]
    mixed_t, slope, x_freq, k_freq = conv_forward(mix_t, kernel, state_term, skip_column)

    if split == 1:
        glu_t = mixed_t
    else:
        glu_t = to_rows(mixed_t.T).T
    pre_glu = jnp.einsum("hl,he->le", glu_t, glu_full, preferred_element_type=F32)
    value = pre_glu[:, :width]
    gate = jax.nn.sigmoid(pre_glu[:, width:])
    halfway = tok + value * gate
    half_normal, half_inv = norm_parts(halfway)
    ffn_x = (half_normal * preffn_gain).astype(BF16)
    ffn_xt = ffn_x.T

    if paired:
        hidden = ffn_in.shape[1]
        first = ffn(ffn_x, ffn_xt, cotangent, ffn_in, ffn_out, pairs.order)
        second = ffn(
            ffn_x,
            ffn_xt,
            cotangent,
            jnp.concatenate(in_pieces, axis=1),
            jnp.concatenate(out_pieces, axis=0),
            jnp.arange(4, dtype=jnp.int32),
        )
        branch = first[0] + second[0]
        d_ffn_x = first[1] + second[1]
    else:
        in_full = lax.all_gather(ffn_in, "mp", axis=1, tiled=True)
        out_full = lax.all_gather(ffn_out, "mp", axis=0, tiled=True)
        count = in_full.shape[1] // 512
        branch, d_ffn_x, d_in, d_out = ffn(
            ffn_x, ffn_xt, cotangent, in_full, out_full, jnp.arange(count, dtype=jnp.int32)
        )
        d_in = jnp.swapaxes(d_in, 0, 1).reshape(width, -1).astype(F32)
        d_out = d_out.reshape(-1, width).astype(F32)
    layer_out = (halfway + branch).astype(BF16)

    grad_preffn = jnp.sum(d_ffn_x * half_normal, axis=0)
    d_half = cotangent.astype(F32) + norm_back(half_normal, half_inv, preffn_gain, d_ffn_x)
    d_value = d_half * gate
    d_gate = d_value * value * (1.0 - gate)
    d_pre = jnp.concatenate([d_value, d_gate], axis=1).astype(BF16)
    d_glu_t = jnp.einsum("he,le->hl", glu_full, d_pre, preferred_element_type=F32)
    d_glu_weight = jnp.einsum("hl,le->he", glu_t, d_pre, preferred_element_type=F32)

    d_mixed_t = d_glu_t if split == 1 else to_channels(d_glu_t.T.astype(BF16)).T
    d_mix_t, d_kernel, d_y, d_skip = conv_backward(d_mixed_t, slope, mix_t, x_freq, k_freq, skip_column)
    sums = moments(lam, d_kernel, d_y)
    grad_step, grad_decay, grad_freq, grad_out, grad_prior = mode_grads(terms, sums, my_step, my_decay, my_freq)
    grad_skip = d_skip[:, 0]
    d_mixin = to_rows(d_mix_t.T).astype(F32)
    grad_premix = jnp.sum(d_mixin * normal, axis=0)
    tokens_grad = d_half + norm_back(normal, inv, premix_gain, d_mixin)

    if paired:
        ffn_in_sum = pairs.place(pairs.reduce(first[2], second[2]), 1)
        ffn_out_sum = pairs.place(pairs.reduce(first[3], second[3]), 0)
        low = d_glu_weight.astype(BF16).reshape(2, 4, quarter, 2 * width)
        halves = [
            jnp.stack([lax.dynamic_slice(low, (side, pairs.order[at], 0, 0), (1, 1) + low.shape[2:])[0, 0] for at in range(4)])
            for side in (mp, 1 - mp)
        ]
        glu_sum = pairs.place(pairs.reduce(*halves), 0)

        per_mode = jnp.concatenate([grad_decay[None], grad_freq[None], grad_out, ]).reshape(4, 2, shard, modes)
        per_channel = jnp.stack([grad_step, grad_skip]).reshape(2, 2, shard)
        norms = jnp.stack([grad_premix, grad_preffn])

        def pack(side):
            parts = [
                lax.dynamic_index_in_dim(per_mode, side, 1, False),
                lax.dynamic_index_in_dim(per_channel, side, 1, False),
                norms,
            ]
            return jnp.concatenate([p.reshape(-1, LANES) for p in parts], axis=0)

        small = pairs.sum_small(pack(mp) + pairs.swap_y(pack(1 - mp)))
        flat = small.reshape(-1)
        sizes = [4 * shard * modes, 2 * shard, 2 * width]
        mode_sum = flat[: sizes[0]].reshape(4, shard, modes)
        channel_sum = flat[sizes[0] : sizes[0] + sizes[1]].reshape(2, shard)
        norm_sum = flat[sizes[0] + sizes[1] :].reshape(2, width)
        decay_sum, freq_sum, out_sum = mode_sum[0], mode_sum[1], mode_sum[2:]
        step_sum, skip_sum = channel_sum[0], channel_sum[1]
        premix_sum, preffn_sum = norm_sum[0], norm_sum[1]

        sides = grad_prior.reshape(2, 2, shard, modes)
        keep = lax.dynamic_index_in_dim(sides, mp, 1, False)
        got = pairs.swap_y(lax.dynamic_index_in_dim(sides, 1 - mp, 1, False))
        state_grad = jnp.stack([jnp.where(mp == 0, keep, got), jnp.where(mp == 0, got, keep)], axis=1)
    else:
        segments = prior_state.shape[1]

        def over_all(v, axis):
            shape = list(v.shape)
            shape[axis] = width
            every = lax.dynamic_update_slice_in_dim(jnp.zeros(shape, F32), v, (mp % split) * channels, axis)
            every = lax.psum(every, ("dp", "mp"))
            return lax.dynamic_slice_in_dim(every, mp * shard, shard, axis)

        decay_sum, freq_sum = over_all(grad_decay, 0), over_all(grad_freq, 0)
        out_sum, step_sum, skip_sum = over_all(grad_out, 1), over_all(grad_step, 0), over_all(grad_skip, 0)
        premix_sum, preffn_sum = lax.psum((grad_premix, grad_preffn), ("dp", "mp"))
        every = jnp.zeros((2, segments, width, modes), F32)
        every = lax.dynamic_update_slice(every, grad_prior[:, None], (0, mp // split, (mp % split) * channels, 0))
        every = lax.psum(every, "mp")
        state_grad = lax.dynamic_slice_in_dim(every, mp * shard, shard, 2)
        scatter = lambda v, axis: lax.psum(lax.psum_scatter(v, "mp", scatter_dimension=axis, tiled=True), "dp")
        glu_sum, ffn_in_sum, ffn_out_sum = scatter(d_glu_weight, 0), scatter(d_in, 1), scatter(d_out, 0)

    return (
        layer_out,
        tokens_grad,
        premix_sum,
        step_sum,
        decay_sum,
        freq_sum,
        out_sum,
        skip_sum,
        state_grad,
        glu_sum,
        preffn_sum,
        ffn_in_sum,
        ffn_out_sum,
    )


def solution(mesh):
    placed = (
        P(("dp", "mp"), None),
        P(),
        P("mp"),
        P("mp", None),
        P("mp", None),
        P(None, "mp", None),
        P("mp"),
        P(None, "dp", "mp", None),
        P("mp", None),
        P(),
        P(None, "mp"),
        P("mp", None),
        P(("dp", "mp"), None),
    )
    return jax.shard_map(
        local,
        mesh=mesh,
        in_specs=placed,
        out_specs=(
            P(("dp", "mp"), None),
            P(("dp", "mp"), None),
            P(),
            P("mp"),
            P("mp", None),
            P("mp", None),
            P(None, "mp", None),
            P("mp"),
            P(None, "dp", "mp", None),
            P("mp", None),
            P(),
            P(None, "mp"),
            P("mp", None),
        ),
        check_vma=False,
    )
```

time: 4530 us -> 724 us (0.16)
  matrix products: 3450 us -> 22.3 us
  waiting for transfers between devices: 802 us -> 208 us
  Pallas kernels: 0 us -> 202 us
  starting transfers between devices: 0.37 us -> 78.4 us
  blocking collectives: 74 us -> 0 us
    dot_general x31 -> x3, matrix products: 3450 us -> 22.3 us  [the longest x1 8.19 us: local(): jnp.einsum('he,le->hl', glu_full, d_pre, preferred_element_type=F32)]
    reduce_scatter x4 -> x0, waiting for transfers between devices: 373 us -> none  [the longest x1 192 us: local(): lax.psum_scatter(jnp.dot(glu_in, glu_weight, preferred_element_type=jnp.f...]
    psum x1 -> x0, waiting for transfers between devices: 287 us -> none  [local(): lax.psum((grad_glu, grad_ffn_in, grad_ffn_out, grad_step, grad_decay, gra...]
    ppermute x0 -> x59, waiting for transfers between devices: none -> 208 us  [the longest x9 85.9 us: swap_x(): return lax.ppermute(v, 'dp', [(i, i ^ 2) for i in range(self.dp_size)])]
    pallas_call x0 -> x6, Pallas kernels: none -> 202 us  [the longest x2 76.7 us: ffn(): pl.pallas_call(ffn_kernel, grid_spec=pltpu.PrefetchScalarGridSpec(num_sca...]
    all_gather x4 -> x0, waiting for transfers between devices: 141 us -> none  [the longest x1 75.2 us: local(): grad_pre_rows = lax.all_gather(grad_pre, 'mp', axis=0, tiled=True)]
    ppermute x0 -> x59, starting transfers between devices: none -> 78.4 us  [the longest x18 51.7 us: shift_z(): lax.ppermute(v, 'dp', [(i, (i + 4 * by) % self.dp_size) for i in range(se...]
    psum x2 -> x0, blocking collectives: 74 us -> none  [the longest x1 38.6 us: local(): lax.psum((grad_premix, grad_preffn), ('dp', 'mp'))]
  transfers between devices with their start and end apart: 9 -> 59, of which waited for: 7 -> 22; matrix products, arithmetic and copies ran while one was open for 59% -> 29% of each run, Pallas kernels for 0% -> 28%
where the time goes in v1:
time: 724 us; the launch traced here: 713 us
  waiting for transfers between devices  208 us (29%)
  Pallas kernels  202 us (28%)
  local copies, waits for them, and re-layouts  117 us (16%)
  other arithmetic  81.8 us (11%)
  starting transfers between devices  78.4 us (11%)
  matrix products  22.3 us (3%)
    ppermute x9, waiting for transfers between devices, swap_x(): return lax.ppermute(v, 'dp', [(i, i ^ 2) for i in range(self.dp_size)])  85.9 us
    pallas_call x2, Pallas kernels, ffn(): pl.pallas_call(ffn_kernel, grid_spec=pltpu.PrefetchScalarGridSpec(num_sca...  76.7 us
    ppermute x9, waiting for transfers between devices, swap_y(): return lax.ppermute(v, 'mp', [(0, 1), (1, 0)])  64.7 us
    ppermute x18, starting transfers between devices, shift_z(): lax.ppermute(v, 'dp', [(i, (i + 4 * by) % self.dp_size) for i in range(se...  51.7 us
    pallas_call x1, Pallas kernels, conv_forward(): pl.pallas_call(conv_forward_kernel, grid=(channels // block,), in_specs=[...  49 us
    ppermute x18, waiting for transfers between devices, shift_z(): lax.ppermute(v, 'dp', [(i, (i + 4 * by) % self.dp_size) for i in range(se...  47 us
    unnamed x143, local copies, waits for them, and re-layouts  31.1 us
    pallas_call x1, Pallas kernels, moments(): pl.pallas_call(moments_kernel, grid=(groups // 8,), in_specs=[spec, spec,...  28.4 us
  transfers between devices with their start and end apart: 59, of which 22 were waited for; matrix products, arithmetic and copies ran while one was open for 29% of the time, Pallas kernels for 28%

profile of v1, /device:TPU:0, one launch (start us, length us, event | category | flops | bytes accessed | tf_op | source)
XLA Modules:
  0.0 712.7 jit_solution(424983226563017688)
XLA Ops:
  45.4 25.6 %synth.1 = (f32[1024,1024]{1,0:T(8,128)}, f32[1024,1024]{1,0:T(8,128)}) custom-call(f32[256,128]{1,0:T(8,128)} %get-tuple-element.141.lr, f32[256,128]{1,0:T(8,128)} %get-tuple-element.140.li, f32[256,128]{1,0:T(8,128)} %get-tuple-element.193.kr, f32[256,128]{1,0:T(8,128)} %get-tuple-element.192.ki, f32[256,128]{1,0:T(8,128)} %subtract_multiply_fusion.2.wr, ...), custom_call_target="tpu_custom_call" | custom-call | flops 17999998976 | tf_op jit(solution)/shard_map/synth/pallas_call | solution.py:162
  74.0 49.0 %conv_forward.1 = (bf16[1024,1024]{1,0:T(8,128)(2,1)}, f32[1024,1024]{1,0:T(8,128)}, bf16[1024,2048]{1,0:T(8,128)(2,1)}, bf16[1024,2048]{1,0:T(8,128)(2,1)}) custom-call(bf16[1024,1024]{1,0:T(8,128)(2,1)} %fusion.19.x_ref, f32[1024,1024]{1,0:T(8,128)} %get-tuple-element.39.k_ref, f32[1024,1024]{1,0:T(8,128)} %get-tuple-element.40.st_ref, ...), custom_call_target="tpu_custom_call" | custom-call | flops 35999997952 | tf_op jit(solution)/shard_map/conv_forward/pallas_call | solution.py:286
  133.0 6.6 fusion.57
  152.4 21.6 %collective-permute-done.10 = bf16[512,1024]{1,0:T(8,128)(2,1)} collective-permute-done((bf16[512,1024]{1,0:T(8,128)(2,1)}, bf16[512,1024]{1,0:T(8,128)(2,1)}, u32[]{:S(2)}, u32[]{:S(2)}) %collective-permute-start.10) | collective-permute-done | bytes 1048608 | tf_op jit(solution)/shard_map/ppermute | solution.py:435
  174.0 38.1 %ffn.2 = (f32[1024,1024]{1,0:T(8,128)}, f32[1024,1024]{1,0:T(8,128)}, bf16[4,1024,512]{2,1,0:T(8,128)(2,1)}, bf16[4,512,1024]{2,1,0:T(8,128)(2,1)}) custom-call(s32[4]{0:T(128)} %pad_add_fusion.order, bf16[1024,1024]{1,0:T(8,128)(2,1)} %copy.141.x_ref, bf16[1024,1024]{1,0:T(8,128)(2,1)} %fusion.62.xt_ref, bf16[1024,1024]{1,0:T(8,128)(2,1)} %c_ref.3, ...), custom_call_target="tpu_custom_call" | custom-call | flops 32399998976 | tf_op jit(solution)/shard_map/ffn/pallas_call | solution.py:386
  217.4 5.4 copy.146
  222.7 5.3 copy.143
  235.6 38.6 %ffn.3 = (f32[1024,1024]{1,0:T(8,128)}, f32[1024,1024]{1,0:T(8,128)}, bf16[4,1024,512]{2,1,0:T(8,128)(2,1)}, bf16[4,512,1024]{2,1,0:T(8,128)(2,1)}) custom-call(s32[4]{0:T(128)} %iota.3.order, bf16[1024,1024]{1,0:T(8,128)(2,1)} %copy.141.x_ref, bf16[1024,1024]{1,0:T(8,128)(2,1)} %fusion.62.xt_ref, bf16[1024,1024]{1,0:T(8,128)(2,1)} %c_ref.3, ...), custom_call_target="tpu_custom_call" | custom-call | flops 32399998976 | tf_op jit(solution)/shard_map/ffn/pallas_call | solution.py:386
  274.2 5.3 copy.147
  279.5 5.3 copy.144
  284.9 6.4 multiply_reduce_fusion
  291.4 8.0 %multiply_convert_fusion.2 = (bf16[1024,1024]{0,1:T(8,128)(2,1)}, f32[1024,1024]{0,1:T(8,128)S(1)}, bf16[1024,1024]{0,1:T(8,128)(2,1)}) fusion(f32[1024,2048]{0,1:T(8,128)} %copy-done.4, f32[1024]{0:T(1024)S(1)} %get-tuple-element.201, f32[1024,1024]{0,1:T(8,128)S(1)} %copy-done.1, f32[1024]{0:T(1024)S(1)} %broadcast_multiply_fusion.7, ...), kind=kLoop, calls=%fused_computation.59 | loop fusion | flops 17825792 | bytes 31477760 | tf_op jit(solution)/shard_map/convert.7
  303.2 7.6 %convolution_convert_fusion = bf16[1024,2048]{1,0:T(8,128)(2,1)} fusion(bf16[1024,1024]{1,0:T(8,128)(2,1)S(1)} %copy-done.62, bf16[1024,1024]{0,1:T(8,128)(2,1)S(1)} %multiply_convert_fusion, bf16[1024,1024]{0,1:T(8,128)(2,1)S(1)} %copy-done.28), kind=kOutput, calls=%fused_computation.40 | convolution fusion | flops 4305453056 | bytes 10485760 | tf_op jit(solution)/shard_map/hl,le->he/dot_general | solution.py:668
  310.7 8.2 %fusion.18.g_ref = f32[1024,1024]{1,0:T(8,128)} fusion(bf16[1024,2048]{1,0:T(8,128)(2,1)} %constant_dynamic-update-slice_fusion, bf16[1024,1024]{0,1:T(8,128)(2,1)S(1)} %multiply_convert_fusion, bf16[1024,1024]{0,1:T(8,128)(2,1)S(1)} %copy-done.28), kind=kOutput, calls=%fused_computation.42 | convolution fusion | flops 4303355904 | bytes 12582912 | tf_op jit(solution)/shard_map/he,le->hl/dot_general | solution.py:667
  318.9 22.5 %conv_backward.1 = (bf16[1024,1024]{1,0:T(8,128)(2,1)}, bf16[1024,1024]{1,0:T(8,128)(2,1)}, bf16[1024,1024]{1,0:T(8,128)(2,1)}, f32[1024,1]{1,0:T(8,128)}) custom-call(f32[1024,1024]{1,0:T(8,128)} %fusion.18.g_ref, f32[1024,1024]{1,0:T(8,128)} %get-tuple-element.46.slope_ref, bf16[1024,1024]{1,0:T(8,128)(2,1)} %fusion.19.x_ref, ...), custom_call_target="tpu_custom_call" | custom-call | flops 19800000512 | tf_op jit(solution)/shard_map/conv_backward/pallas_call | solution.py:331
  341.5 28.4 %moments.1 = (f32[256,128]{1,0:T(8,128)}, f32[256,128]{1,0:T(8,128)}, f32[256,128]{1,0:T(8,128)}, f32[256,128]{1,0:T(8,128)}, f32[256,128]{1,0:T(8,128)}, /*inde...) custom-call(f32[256,128]{1,0:T(8,128)} %get-tuple-element.141.lr, f32[256,128]{1,0:T(8,128)} %get-tuple-element.140.li, ...), custom_call_target="tpu_custom_call" | custom-call | flops 22499999744 | tf_op jit(solution)/shard_map/moments/pallas_call | solution.py:235
  410.7 4.8 collective-permute-done.15
  426.9 5.4 fusion.10
  436.7 5.5 copy.163
  453.2 12.5 %collective-permute-done.23 = bf16[128,2048]{1,0:T(8,128)(2,1)S(1)} collective-permute-done((bf16[128,2048]{1,0:T(8,128)(2,1)S(1)}, bf16[128,2048]{1,0:T(8,128)(2,1)S(1)}, u32[]{:S(2)}, u32[]{:S(2)}) %collective-permute-start.23) | collective-permute-done | bytes 524320 | tf_op jit(solution)/shard_map/ppermute | solution.py:435
  489.6 7.0 collective-permute-done.28
  502.8 24.2 %collective-permute-done.48 = bf16[2,512,1024]{2,1,0:T(8,128)(2,1)} collective-permute-done((bf16[2,512,1024]{2,1,0:T(8,128)(2,1)S(1)}, bf16[2,512,1024]{2,1,0:T(8,128)(2,1)}, u32[]{:S(2)}, u32[]{:S(2)}) %collective-permute-start.48) | collective-permute-done | bytes 2097184 | tf_op jit(solution)/shard_map/ppermute | solution.py:429
  532.0 38.9 %collective-permute-done.35 = bf16[2,1024,512]{2,1,0:T(8,128)(2,1)} collective-permute-done((bf16[2,1024,512]{2,1,0:T(8,128)(2,1)}, bf16[2,1024,512]{2,1,0:T(8,128)(2,1)}, u32[]{:S(2)}, u32[]{:S(2)}) %collective-permute-start.35) | collective-permute-done | bytes 2097184 | tf_op jit(solution)/shard_map/ppermute | solution.py:429
  579.4 18.9 %collective-permute-done.36 = bf16[1024,512]{1,0:T(8,128)(2,1)S(1)} collective-permute-done((bf16[1024,512]{1,0:T(8,128)(2,1)S(1)}, bf16[1024,512]{1,0:T(8,128)(2,1)S(1)}, u32[]{:S(2)}, u32[]{:S(2)}) %collective-permute-start.36) | collective-permute-done | bytes 1048608 | tf_op jit(solution)/shard_map/ppermute | solution.py:435
  601.7 11.7 %collective-permute-done.52 = bf16[128,1024]{1,0:T(8,128)(2,1)S(1)} collective-permute-done((bf16[128,1024]{1,0:T(8,128)(2,1)S(1)}, bf16[128,1024]{1,0:T(8,128)(2,1)S(1)}, u32[]{:S(2)}, u32[]{:S(2)}) %collective-permute-start.52) | collective-permute-done | bytes 262176 | tf_op jit(solution)/shard_map/ppermute | solution.py:438
  615.9 5.5 collective-permute-start.54
  624.0 15.6 %collective-permute-start.55 = (bf16[128,1024]{1,0:T(8,128)(2,1)S(1)}, bf16[128,1024]{1,0:T(8,128)(2,1)S(1)}, u32[]{:S(2)}, u32[]{:S(2)}) collective-permute-start(bf16[128,1024]{1,0:T(8,128)(2,1)S(1)} %get-tuple-element.124), channel_id=1, source_target_pairs={{0,24},{2,26},{4,28},{6,30},{8,0},{10,2},{12,4},{14,6},{16,8},{18,... | collective-permute-start | bytes 786440 | tf_op jit(solution)/shard_map/ppermute | solution.py:438
  642.5 6.0 collective-permute-start.41
  648.5 7.1 %collective-permute-done.54 = bf16[128,1024]{1,0:T(8,128)(2,1)S(1)} collective-permute-done((bf16[128,1024]{1,0:T(8,128)(2,1)S(1)}, bf16[128,1024]{1,0:T(8,128)(2,1)S(1)}, u32[]{:S(2)}, u32[]{:S(2)}) %collective-permute-start.54) | collective-permute-done | bytes 262176 | tf_op jit(solution)/shard_map/ppermute | solution.py:438
  660.0 6.9 collective-permute-done.41
  672.0 13.7 %collective-permute-done.56 = bf16[512,1024]{1,0:T(8,128)(2,1)S(1)} collective-permute-done((bf16[512,1024]{1,0:T(8,128)(2,1)S(1)}, bf16[512,1024]{1,0:T(8,128)(2,1)S(1)}, u32[]{:S(2)}, u32[]{:S(2)}) %collective-permute-start.56) | collective-permute-done | bytes 1048608 | tf_op jit(solution)/shard_map/ppermute | solution.py:435
  685.7 19.0 %collective-permute-done.43 = bf16[1024,512]{1,0:T(8,128)(2,1)S(1)} collective-permute-done((bf16[1024,512]{1,0:T(8,128)(2,1)S(1)}, bf16[1024,512]{1,0:T(8,128)(2,1)S(1)}, u32[]{:S(2)}, u32[]{:S(2)}) %collective-permute-start.43) | collective-permute-done | bytes 1048608 | tf_op jit(solution)/shard_map/ppermute | solution.py:435
  (428 shorter events, 225.4 us)
Async XLA Ops:
  3.8 26.3 %collective-permute-start = (f32[3104,32]{0,1:T(8,128)S(1)}, f32[3104,32]{0,1:T(8,128)S(1)}, u32[]{:S(2)}, u32[]{:S(2)}) collective-permute-start(f32[3104,32]{0,1:T(8,128)S(1)} %concatenate.49), channel_id=1, source_target_pairs={{0,1},{1,0},{2,3},{3,2},{4,5},{5,4},{6,7},{7,6},{8,9},{9,8},{10,11... | collective-permute-start | bytes 1191944 | tf_op jit(solution)/shard_map/ppermute | solution.py:429
  8.7 63.3 %collective-permute-start.1 = (bf16[128,2048]{1,0:T(8,128)(2,1)}, bf16[128,2048]{1,0:T(8,128)(2,1)}, u32[]{:S(2)}, u32[]{:S(2)}) collective-permute-start(bf16[128,2048]{1,0:T(8,128)(2,1)} %constant_dynamic-slice_fusion.7), channel_id=1, source_target_pairs={{0,1},{1,0},{2,3},{3,2},{4,5},{5,4},{6,7},{7,6},{8,9},{9,8},{10,11... | collective-permute-start | bytes 1572872 | tf_op jit(solution)/shard_map/ppermute | solution.py:429
  11.0 115.1 %collective-permute-start.5 = (bf16[1024,512]{1,0:T(8,128)(2,1)}, bf16[1024,512]{1,0:T(8,128)(2,1)}, u32[]{:S(2)}, u32[]{:S(2)}) collective-permute-start(bf16[1024,512]{1,0:T(8,128)(2,1)} %constant_dynamic-slice_fusion.6), channel_id=1, source_target_pairs={{0,1},{1,0},{2,3},{3,2},{4,5},{5,4},{6,7},{7,6},{8,9},{9,8},{10,11... | collective-permute-start | bytes 3145736 | tf_op jit(solution)/shard_map/ppermute | solution.py:429
  15.3 110.9 %collective-permute-start.9 = (bf16[512,1024]{1,0:T(8,128)(2,1)}, bf16[512,1024]{1,0:T(8,128)(2,1)}, u32[]{:S(2)}, u32[]{:S(2)}) collective-permute-start(bf16[512,1024]{1,0:T(8,128)(2,1)} %constant_dynamic-slice_fusion.5), channel_id=1, source_target_pairs={{0,1},{1,0},{2,3},{3,2},{4,5},{5,4},{6,7},{7,6},{8,9},{9,8},{10,11... | collective-permute-start | bytes 3145736 | tf_op jit(solution)/shard_map/ppermute | solution.py:429
  72.0 51.6 %collective-permute-start.2 = (bf16[128,2048]{1,0:T(8,128)(2,1)}, bf16[128,2048]{1,0:T(8,128)(2,1)}, u32[]{:S(2)}, u32[]{:S(2)}) collective-permute-start(bf16[128,2048]{1,0:T(8,128)(2,1)} %collective-permute-done.1), channel_id=1, source_target_pairs={{0,4},{2,6},{4,0},{6,2},{8,12},{10,14},{12,8},{14,10},{16,20},{18,... | collective-permute-start | bytes 1572872 | tf_op jit(solution)/shard_map/ppermute | solution.py:435
  74.0 56.1 %collective-permute-start.3 = (bf16[128,2048]{1,0:T(8,128)(2,1)}, bf16[128,2048]{1,0:T(8,128)(2,1)}, u32[]{:S(2)}, u32[]{:S(2)}) collective-permute-start(bf16[128,2048]{1,0:T(8,128)(2,1)} %collective-permute-done.1), channel_id=1, source_target_pairs={{0,2},{2,0},{4,6},{6,4},{8,10},{10,8},{12,14},{14,12},{16,18},{18,... | collective-permute-start | bytes 1572872 | tf_op jit(solution)/shard_map/ppermute | solution.py:432
  126.1 26.2 %collective-permute-start.6 = (bf16[1024,512]{1,0:T(8,128)(2,1)}, bf16[1024,512]{1,0:T(8,128)(2,1)S(1)}, u32[]{:S(2)}, u32[]{:S(2)}) collective-permute-start(bf16[1024,512]{1,0:T(8,128)(2,1)} %collective-permute-done.5), channel_id=1, source_target_pairs={{0,4},{2,6},{4,0},{6,2},{8,12},{10,14},{12,8},{14,10},{16,20},{18,... | collective-permute-start | bytes 3145736 | tf_op jit(solution)/shard_map/ppermute | solution.py:435
  126.2 101.9 %collective-permute-start.7 = (bf16[1024,512]{1,0:T(8,128)(2,1)}, bf16[1024,512]{1,0:T(8,128)(2,1)}, u32[]{:S(2)}, u32[]{:S(2)}) collective-permute-start(bf16[1024,512]{1,0:T(8,128)(2,1)} %collective-permute-done.5), channel_id=1, source_target_pairs={{0,2},{2,0},{4,6},{6,4},{8,10},{10,8},{12,14},{14,12},{16,18},{18,... | collective-permute-start | bytes 3145736 | tf_op jit(solution)/shard_map/ppermute | solution.py:432
  126.2 47.8 %collective-permute-start.10 = (bf16[512,1024]{1,0:T(8,128)(2,1)}, bf16[512,1024]{1,0:T(8,128)(2,1)}, u32[]{:S(2)}, u32[]{:S(2)}) collective-permute-start(bf16[512,1024]{1,0:T(8,128)(2,1)} %collective-permute-done.9), channel_id=1, source_target_pairs={{0,4},{2,6},{4,0},{6,2},{8,12},{10,14},{12,8},{14,10},{16,20},{18,... | collective-permute-start | bytes 3145736 | tf_op jit(solution)/shard_map/ppermute | solution.py:435
  130.0 101.5 %collective-permute-start.11 = (bf16[512,1024]{1,0:T(8,128)(2,1)}, bf16[512,1024]{1,0:T(8,128)(2,1)}, u32[]{:S(2)}, u32[]{:S(2)}) collective-permute-start(bf16[512,1024]{1,0:T(8,128)(2,1)} %collective-permute-done.9), channel_id=1, source_target_pairs={{0,2},{2,0},{4,6},{6,4},{8,10},{10,8},{12,14},{14,12},{16,18},{18,... | collective-permute-start | bytes 3145736 | tf_op jit(solution)/shard_map/ppermute | solution.py:432
  152.4 75.7 %collective-permute-start.8 = (bf16[1024,512]{1,0:T(8,128)(2,1)S(1)}, bf16[1024,512]{1,0:T(8,128)(2,1)S(1)}, u32[]{:S(2)}, u32[]{:S(2)}) collective-permute-start(bf16[1024,512]{1,0:T(8,128)(2,1)S(1)} %collective-permute-done.6), channel_id=1, source_target_pairs={{0,2},{2,0},{4,6},{6,4},{8,10},{10,8},{12,14},{14,12},{16,18},{18,... | collective-permute-start | bytes 3145736 | tf_op jit(solution)/shard_map/ppermute | solution.py:432
  174.0 57.6 %collective-permute-start.12 = (bf16[512,1024]{1,0:T(8,128)(2,1)}, bf16[512,1024]{1,0:T(8,128)(2,1)S(1)}, u32[]{:S(2)}, u32[]{:S(2)}) collective-permute-start(bf16[512,1024]{1,0:T(8,128)(2,1)} %collective-permute-done.10), channel_id=1, source_target_pairs={{0,2},{2,0},{4,6},{6,4},{8,10},{10,8},{12,14},{14,12},{16,18},{18,... | collective-permute-start | bytes 3145736 | tf_op jit(solution)/shard_map/ppermute | solution.py:432
  215.4 287.4 %collective-permute-start.46 = (bf16[2,512,1024]{2,1,0:T(8,128)(2,1)}, bf16[2,512,1024]{2,1,0:T(8,128)(2,1)}, u32[]{:S(2)}, u32[]{:S(2)}) collective-permute-start(bf16[2,512,1024]{2,1,0:T(8,128)(2,1)} %slice.175), channel_id=1, source_target_pairs={{0,2},{2,0},{4,6},{6,4},{8,10},{10,8},{12,14},{14,12},{16,18},{18,... | collective-permute-start | bytes 6291464 | tf_op jit(solution)/shard_map/ppermute | solution.py:432
  404.7 44.5 %collective-permute-start.20 = (bf16[2,128,2048]{2,1,0:T(8,128)(2,1)}, bf16[2,128,2048]{2,1,0:T(8,128)(2,1)}, u32[]{:S(2)}, u32[]{:S(2)}) collective-permute-start(bf16[2,128,2048]{2,1,0:T(8,128)(2,1)} %pad_maximum_fusion.5), channel_id=1, source_target_pairs={{0,2},{2,0},{4,6},{6,4},{8,10},{10,8},{12,14},{14,12},{16,18},{18,... | collective-permute-start | bytes 3145736 | tf_op jit(solution)/shard_map/ppermute | solution.py:432
  407.5 38.1 %collective-permute-start.19 = (f32[2,512,32]{1,2,0:T(8,128)}, f32[2,512,32]{1,2,0:T(8,128)}, u32[]{:S(2)}, u32[]{:S(2)}) collective-permute-start(f32[2,512,32]{1,2,0:T(8,128)} %fusion.36), channel_id=1, source_target_pairs={{0,1},{1,0},{2,3},{3,2},{4,5},{5,4},{6,7},{7,6},{8,9},{9,8},{10,11... | collective-permute-start | bytes 393224 | tf_op jit(solution)/shard_map/ppermute | solution.py:429
  449.1 33.4 %collective-permute-start.34 = (bf16[2,1024,512]{2,1,0:T(8,128)(2,1)}, bf16[2,1024,512]{2,1,0:T(8,128)(2,1)S(1)}, u32[]{:S(2)}, u32[]{:S(2)}) collective-permute-start(bf16[2,1024,512]{2,1,0:T(8,128)(2,1)} %slice.171), channel_id=1, source_target_pairs={{0,2},{2,0},{4,6},{6,4},{8,10},{10,8},{12,14},{14,12},{16,18},{18,... | collective-permute-start | bytes 6291464 | tf_op jit(solution)/shard_map/ppermute | solution.py:432
  474.2 57.8 %collective-permute-start.33 = (bf16[2,1024,512]{2,1,0:T(8,128)(2,1)}, bf16[2,1024,512]{2,1,0:T(8,128)(2,1)}, u32[]{:S(2)}, u32[]{:S(2)}) collective-permute-start(bf16[2,1024,512]{2,1,0:T(8,128)(2,1)} %slice.169), channel_id=1, source_target_pairs={{0,2},{2,0},{4,6},{6,4},{8,10},{10,8},{12,14},{14,12},{16,18},{18,... | collective-permute-start | bytes 6291464 | tf_op jit(solution)/shard_map/ppermute | solution.py:432
  478.4 48.6 %collective-permute-start.48 = (bf16[2,512,1024]{2,1,0:T(8,128)(2,1)S(1)}, bf16[2,512,1024]{2,1,0:T(8,128)(2,1)}, u32[]{:S(2)}, u32[]{:S(2)}) collective-permute-start(bf16[2,512,1024]{2,1,0:T(8,128)(2,1)S(1)} %add_convert_fusion.1), channel_id=1, source_target_pairs={{0,1},{1,0},{2,3},{3,2},{4,5},{5,4},{6,7},{7,6},{8,9},{9,8},{10,11... | collective-permute-start | bytes 6291464 | tf_op jit(solution)/shard_map/ppermute | solution.py:429
  484.4 86.5 %collective-permute-start.35 = (bf16[2,1024,512]{2,1,0:T(8,128)(2,1)}, bf16[2,1024,512]{2,1,0:T(8,128)(2,1)}, u32[]{:S(2)}, u32[]{:S(2)}) collective-permute-start(bf16[2,1024,512]{2,1,0:T(8,128)(2,1)} %add_convert_fusion.4), channel_id=1, source_target_pairs={{0,1},{1,0},{2,3},{3,2},{4,5},{5,4},{6,7},{7,6},{8,9},{9,8},{10,11... | collective-permute-start | bytes 6291464 | tf_op jit(solution)/shard_map/ppermute | solution.py:429
  502.2 73.1 %collective-permute-start.30 = (bf16[128,2048]{1,0:T(8,128)(2,1)S(1)}, bf16[128,2048]{1,0:T(8,128)(2,1)S(1)}, u32[]{:S(2)}, u32[]{:S(2)}) collective-permute-start(bf16[128,2048]{1,0:T(8,128)(2,1)S(1)} %bitcast.213), channel_id=1, source_target_pairs={{0,4},{2,6},{4,0},{6,2},{8,12},{10,14},{12,8},{14,10},{16,20},{18,... | collective-permute-start | bytes 1572872 | tf_op jit(solution)/shard_map/ppermute | solution.py:435
  502.8 110.9 %collective-permute-start.31 = (bf16[128,2048]{1,0:T(8,128)(2,1)S(1)}, bf16[128,2048]{1,0:T(8,128)(2,1)S(1)}, u32[]{:S(2)}, u32[]{:S(2)}) collective-permute-start(bf16[128,2048]{1,0:T(8,128)(2,1)S(1)} %bitcast.214), channel_id=1, source_target_pairs={{0,2},{2,0},{4,6},{6,4},{8,10},{10,8},{12,14},{14,12},{16,18},{18,... | collective-permute-start | bytes 1572872 | tf_op jit(solution)/shard_map/ppermute | solution.py:432
  531.4 44.1 %collective-permute-start.49 = (bf16[512,1024]{1,0:T(8,128)(2,1)S(1)}, bf16[512,1024]{1,0:T(8,128)(2,1)S(1)}, u32[]{:S(2)}, u32[]{:S(2)}) collective-permute-start(bf16[512,1024]{1,0:T(8,128)(2,1)S(1)} %slice_bitcast_fusion), channel_id=1, source_target_pairs={{0,4},{2,6},{4,0},{6,2},{8,12},{10,14},{12,8},{14,10},{16,20},{18,... | collective-permute-start | bytes 3145736 | tf_op jit(solution)/shard_map/ppermute | solution.py:435
  575.3 92.9 %collective-permute-start.32 = (bf16[128,2048]{1,0:T(8,128)(2,1)S(1)}, bf16[128,2048]{1,0:T(8,128)(2,1)S(1)}, u32[]{:S(2)}, u32[]{:S(2)}) collective-permute-start(bf16[128,2048]{1,0:T(8,128)(2,1)S(1)} %collective-permute-done.30), channel_id=1, source_target_pairs={{0,2},{2,0},{4,6},{6,4},{8,10},{10,8},{12,14},{14,12},{16,18},{18,... | collective-permute-start | bytes 1572872 | tf_op jit(solution)/shard_map/ppermute | solution.py:432
  576.1 25.1 %collective-permute-start.51 = (bf16[128,1024]{1,0:T(8,128)(2,1)S(1)}, bf16[128,1024]{1,0:T(8,128)(2,1)S(1)}, u32[]{:S(2)}, u32[]{:S(2)}) collective-permute-start(bf16[128,1024]{1,0:T(8,128)(2,1)S(1)} %get-tuple-element.157), channel_id=1, source_target_pairs={{0,16},{2,18},{4,20},{6,22},{8,24},{10,26},{12,28},{14,30},{16,0},... | collective-permute-start | bytes 786440 | tf_op jit(solution)/shard_map/ppermute | solution.py:438
  613.4 26.2 %collective-permute-start.39 = (bf16[256,512]{1,0:T(8,128)(2,1)S(1)}, bf16[256,512]{1,0:T(8,128)(2,1)S(1)}, u32[]{:S(2)}, u32[]{:S(2)}) collective-permute-start(bf16[256,512]{1,0:T(8,128)(2,1)S(1)} %get-tuple-element.159), channel_id=1, source_target_pairs={{0,24},{2,26},{4,28},{6,30},{8,0},{10,2},{12,4},{14,6},{16,8},{18,... | collective-permute-start | bytes 786440 | tf_op jit(solution)/shard_map/ppermute | solution.py:438
  613.7 28.8 %collective-permute-start.53 = (bf16[128,1024]{1,0:T(8,128)(2,1)S(1)}, bf16[128,1024]{1,0:T(8,128)(2,1)S(1)}, u32[]{:S(2)}, u32[]{:S(2)}) collective-permute-start(bf16[128,1024]{1,0:T(8,128)(2,1)S(1)} %get-tuple-element.124), channel_id=1, source_target_pairs={{0,8},{2,10},{4,12},{6,14},{8,16},{10,18},{12,20},{14,22},{16,24},... | collective-permute-start | bytes 786440 | tf_op jit(solution)/shard_map/ppermute | solution.py:438
  615.9 39.8 %collective-permute-start.54 = (bf16[128,1024]{1,0:T(8,128)(2,1)S(1)}, bf16[128,1024]{1,0:T(8,128)(2,1)S(1)}, u32[]{:S(2)}, u32[]{:S(2)}) collective-permute-start(bf16[128,1024]{1,0:T(8,128)(2,1)S(1)} %get-tuple-element.124), channel_id=1, source_target_pairs={{0,16},{2,18},{4,20},{6,22},{8,24},{10,26},{12,28},{14,30},{16,0},... | collective-permute-start | bytes 786440 | tf_op jit(solution)/shard_map/ppermute | solution.py:438
  624.0 35.5 %collective-permute-start.55 = (bf16[128,1024]{1,0:T(8,128)(2,1)S(1)}, bf16[128,1024]{1,0:T(8,128)(2,1)S(1)}, u32[]{:S(2)}, u32[]{:S(2)}) collective-permute-start(bf16[128,1024]{1,0:T(8,128)(2,1)S(1)} %get-tuple-element.124), channel_id=1, source_target_pairs={{0,24},{2,26},{4,28},{6,30},{8,0},{10,2},{12,4},{14,6},{16,8},{18,... | collective-permute-start | bytes 786440 | tf_op jit(solution)/shard_map/ppermute | solution.py:438
  659.6 26.2 %collective-permute-start.56 = (bf16[512,1024]{1,0:T(8,128)(2,1)S(1)}, bf16[512,1024]{1,0:T(8,128)(2,1)S(1)}, u32[]{:S(2)}, u32[]{:S(2)}) collective-permute-start(bf16[512,1024]{1,0:T(8,128)(2,1)S(1)} %bitcast.206), channel_id=1, source_target_pairs={{0,4},{2,6},{4,0},{6,2},{8,12},{10,14},{12,8},{14,10},{16,20},{18,... | collective-permute-start | bytes 3145736 | tf_op jit(solution)/shard_map/ppermute | solution.py:435
  667.4 37.3 %collective-permute-start.43 = (bf16[1024,512]{1,0:T(8,128)(2,1)S(1)}, bf16[1024,512]{1,0:T(8,128)(2,1)S(1)}, u32[]{:S(2)}, u32[]{:S(2)}) collective-permute-start(bf16[1024,512]{1,0:T(8,128)(2,1)S(1)} %bitcast.203), channel_id=1, source_target_pairs={{0,4},{2,6},{4,0},{6,2},{8,12},{10,14},{12,8},{14,10},{16,20},{18,... | collective-permute-start | bytes 3145736 | tf_op jit(solution)/shard_map/ppermute | solution.py:435
  668.4 36.9 %collective-permute-start.57 = (bf16[512,1024]{1,0:T(8,128)(2,1)S(1)}, bf16[512,1024]{1,0:T(8,128)(2,1)S(1)}, u32[]{:S(2)}, u32[]{:S(2)}) collective-permute-start(bf16[512,1024]{1,0:T(8,128)(2,1)S(1)} %bitcast.207), channel_id=1, source_target_pairs={{0,2},{2,0},{4,6},{6,4},{8,10},{10,8},{12,14},{14,12},{16,18},{18,... | collective-permute-start | bytes 3145736 | tf_op jit(solution)/shard_map/ppermute | solution.py:432
  668.5 37.0 %collective-permute-start.44 = (bf16[1024,512]{1,0:T(8,128)(2,1)S(1)}, bf16[1024,512]{1,0:T(8,128)(2,1)S(1)}, u32[]{:S(2)}, u32[]{:S(2)}) collective-permute-start(bf16[1024,512]{1,0:T(8,128)(2,1)S(1)} %bitcast.204), channel_id=1, source_target_pairs={{0,2},{2,0},{4,6},{6,4},{8,10},{10,8},{12,14},{14,12},{16,18},{18,... | collective-permute-start | bytes 3145736 | tf_op jit(solution)/shard_map/ppermute | solution.py:432
  (92 other events, 1426.6 us)
